TPU v7x, 256 devices: a whole 4x4x8 slice. The times are simulated.
256 devices in a mesh: dp: 8 (over y, core), vocab: 32 (over z, x).
Axes of the slice: x: 4, y: 4, z: 8, core: 2. Of those that a mesh axis runs over, the one named last changes fastest.
Arguments:
- hidden: bfloat16 [512, 4096], P('dp'), may hold values from -26 to 26
- head_weight: bfloat16 [4096, 151552], P(None, ('dp', 'vocab')), may hold values from -0.3 to 0.3
- teacher_ids: int32 [512, 64], P('dp'), may hold values from 0 to 151551
- teacher_logits: bfloat16 [512, 64], P('dp'), may hold values from -30 to 405
- labels: int32 [512], P('dp'), may hold values from 0 to 151551
- store_ids: int32 [4096, 64], P(('dp', 'vocab')), may hold values from 0 to 151551
- store_logits: bfloat16 [4096, 64], P(('dp', 'vocab')), may hold values from -18 to 18
- owner: int32 [4096, 1], P(('dp', 'vocab')), may hold values from 0 to 7; in each aligned block of 16 rows (0 to 15, 16 to 31, ...) at most 4 rows name the same one
Outputs:
- grad_head: bfloat16 [4096, 151552], P(None, ('dp', 'vocab'))
- grad_hidden: bfloat16 [512, 4096], P('dp', 'vocab')
- token_loss: float32 [512], P('dp')
- next_ids: int32 [8192, 64], P(('dp', 'vocab'))
- next_logits: bfloat16 [8192, 64], P(('dp', 'vocab'))
Inputs may be any that keep to these rules, and one draw needn't show every extreme that they name: Of the 16 rows of one store shard, at most 4 have the same owner, and some shard has exactly 4 rows for one owner.
All inputs are finite; a program needn't handle non-finite values.
Results may differ from a plain program's by a relative error of at most 0.0034.
Values may be sent and summed in bfloat16 or wider, within the bound.
No kernel may reach another device: no remote copies, remote signals or barrier semaphores. Data moves between devices by JAX's collectives and lax.ppermute only.
A program may use at most 64 MiB of HBM per device.

v0:
```python
import functools

import jax
import jax.numpy as jnp
from jax import lax
from jax.experimental import pallas as pl
from jax.experimental.pallas import tpu as pltpu
from jax.sharding import PartitionSpec as P

mixing = 0.5
loss_scale = 64.0
f32 = jnp.float32
bf16 = jnp.bfloat16
NY, NC, NZ, NX = 4, 2, 8, 4
AXES = ("y", "c", "z", "x")
ROWS = 64
TOK = NY * ROWS
D = 4096
COLS = 592
TOPK = 64
CAP = 4
HALF = ROWS // 2
VMEM = 48 * 1024 * 1024
ZSTEP = 4
TARGET_COST = 1_000_000


def index_of(y, c, z, x):
    return (((y % NY) * NC + c % NC) * NZ + z % NZ) * NX + x % NX


def send(value, dy=0, dc=0, dz=0, dx=0):
    pairs = [
        (index_of(y, c, z, x), index_of(y + dy, c + dc, z + dz, x + dx))
        for y in range(NY)
        for c in range(NC)
        for z in range(NZ)
        for x in range(NX)
    ]
    return lax.ppermute(value, AXES, pairs)


def swap_x(value):
    pairs = [
        (index_of(y, c, z, x), index_of(y, c, z, x ^ 1))
        for y in range(NY)
        for c in range(NC)
        for z in range(NZ)
        for x in range(NX)
    ]
    return lax.ppermute(value, AXES, pairs)


def params(size=VMEM):
    return pltpu.CompilerParams(vmem_limit_bytes=size)


def whole():
    return pl.BlockSpec(memory_space=pltpu.VMEM)


def cost(flops, size):
    return pl.CostEstimate(flops=flops, bytes_accessed=size, transcendentals=0)


def pack_kernel(place, owner, ids, scores, label, store_ids, store_logits, *outs):
    y, c = place[2], place[3]
    entries = jnp.concatenate([ids[...].astype(f32), scores[...].astype(f32)], axis=1).T
    teacher = jnp.concatenate([entries[:TOPK], entries[TOPK:]], axis=1)
    label_rows = jnp.concatenate([label[...].astype(f32), jnp.zeros((1, ROWS), f32)], axis=1)
    label_rows = jnp.concatenate([label_rows, jnp.zeros((7, 2 * ROWS), f32)], axis=0)
    lane = lax.broadcasted_iota(jnp.int32, (NC * CAP, 2 * TOPK), 1)
    empty = jnp.where(lane < TOPK, -1.0, 0.0)
    for out in outs:
        out[0:TOPK, :] = teacher
        out[TOPK : TOPK + 8, :] = label_rows
        out[TOPK + 8 : TOPK + 16, :] = empty
    rows = store_ids.shape[0]
    values = jnp.concatenate(
        [store_ids[...].astype(f32), store_logits[...].astype(f32)], axis=1
    )
    for j in range(rows):
        named = owner[j]
        slot = jnp.int32(0)
        for i in range(j):
            slot = slot + (owner[i] == named).astype(jnp.int32)
        ahead = ((named >> 1) + NY - y) & (NY - 1)
        row = TOPK + 8 + ((named + c) & 1) * CAP + slot
        for d in range(NY):

            @pl.when(ahead == d)
            def _(out=outs[d], row=row, j=j):
                out[pl.ds(row, 1), :] = values[j : j + 1, :]


def packs_of(place, owner, ids, scores, label, store_ids, store_logits):
    smem = pl.BlockSpec(memory_space=pltpu.SMEM)
    return pl.pallas_call(
        pack_kernel,
        out_shape=[jax.ShapeDtypeStruct((TOPK + 16, 2 * TOPK), f32)] * NY,
        in_specs=[smem, smem] + [whole()] * 5,
        out_specs=[whole()] * NY,
        compiler_params=params(60 * 1024 * 1024),
        name="pack",
    )(place, owner, ids, scores, label, store_ids, store_logits)


def target_kernel(start_ref, p0, p1, p2, p3, own_ref, par_ref, tk_ref, kept_ref, pass_ref, ids_ref, prob_ref):
    packs = (p0, p1, p2, p3)
    ids_ref[...] = jnp.concatenate([p[0:TOPK, :ROWS] for p in packs], axis=1).astype(jnp.int32)
    scores = jnp.concatenate([p[0:TOPK, ROWS:] for p in packs], axis=1)
    label = jnp.concatenate([p[TOPK : TOPK + 1, :ROWS] for p in packs], axis=1).astype(jnp.int32)
    for d, p in enumerate(packs):
        kept_ref[d * CAP : (d + 1) * CAP, :] = p[TOPK + 8 : TOPK + 8 + CAP, :]
    other = jnp.concatenate([p[TOPK + 8 + CAP : TOPK + 16, :] for p in packs], axis=0)
    named = other[:, :TOPK].astype(jnp.int32)
    digits = [(named >> 16), (named >> 8) & 255, named & 255]
    pass_ref[...] = jnp.concatenate(
        [v.astype(f32) for v in digits] + [other[:, TOPK:]], axis=1
    ).astype(bf16)
    shifted = scores - jnp.max(scores, axis=0, keepdims=True)
    logp = shifted - jnp.log(jnp.sum(jnp.exp(shifted), axis=0, keepdims=True))
    prob = jnp.exp(logp)
    tk_ref[...] = mixing * jnp.sum(prob * logp, axis=0, keepdims=True)
    prob_ref[...] = mixing * prob
    step = 16

    def rows(i, carry):
        first = pl.multiple_of(i * step, step)
        iota = lax.broadcasted_iota(jnp.int32, (step, TOK), 0) + first
        cols_own = iota + start_ref[0]
        cols_par = iota + start_ref[1]
        own = jnp.where(cols_own == label, 1.0 - mixing, 0.0)
        par = jnp.where(cols_par == label, 1.0 - mixing, 0.0)
        for k in range(TOPK):
            ids = ids_ref[pl.ds(k, 1), :]
            p = prob_ref[pl.ds(k, 1), :]
            own = own + jnp.where(cols_own == ids, p, 0.0)
            par = par + jnp.where(cols_par == ids, p, 0.0)
        own_ref[pl.ds(first, step), :] = own
        par_ref[pl.ds(first, step), :] = par
        return carry

    lax.fori_loop(0, COLS // step, rows, 0)


def target_of(start, packs):
    return pl.pallas_call(
        target_kernel,
        out_shape=(
            jax.ShapeDtypeStruct((COLS, TOK), f32),
            jax.ShapeDtypeStruct((COLS, TOK), f32),
            jax.ShapeDtypeStruct((1, TOK), f32),
            jax.ShapeDtypeStruct((NY * CAP, 2 * TOPK), f32),
            jax.ShapeDtypeStruct((NY * CAP, 4 * TOPK), bf16),
        ),
        in_specs=[pl.BlockSpec(memory_space=pltpu.SMEM)] + [whole()] * NY,
        out_specs=(whole(),) * 5,
        scratch_shapes=[pltpu.VMEM((TOPK, TOK), jnp.int32), pltpu.VMEM((TOPK, TOK), f32)],
        compiler_params=params(),
        cost_estimate=cost(TARGET_COST, 1_400_000),
        name="target",
    )(start, *packs)


def unpack_kernel(place, kept, digits, ids, logits, rows):
    y, c = place[2], place[3]
    high, middle, low, scores = (
        digits[:, k * TOPK : (k + 1) * TOPK].astype(f32) for k in range(4)
    )
    passed = jnp.concatenate([high * 65536.0 + (middle * 256.0 + low), scores], axis=1)
    for d in range(NY):
        source = ((y + NY - d) & (NY - 1)) * (NC * CAP)
        at = slice(d * CAP, (d + 1) * CAP)
        rows[pl.ds(source + c * CAP, CAP), :] = kept[at, :]
        rows[pl.ds(source + (1 - c) * CAP, CAP), :] = passed[at]
    ids[...] = rows[:, :TOPK].astype(jnp.int32)
    logits[...] = rows[:, TOPK:].astype(bf16)


def unpacked(place, kept, hid_par):
    rows = NY * NC * CAP
    return pl.pallas_call(
        unpack_kernel,
        out_shape=(
            jax.ShapeDtypeStruct((rows, TOPK), jnp.int32),
            jax.ShapeDtypeStruct((rows, TOPK), bf16),
        ),
        grid=(1,),
        in_specs=[
            pl.BlockSpec(memory_space=pltpu.SMEM),
            pl.BlockSpec((NY * CAP, 2 * TOPK), lambda i: (0, 0)),
            pl.BlockSpec((NY * CAP, 4 * TOPK), lambda i: (TOK // (NY * CAP), 0)),
        ],
        out_specs=(
            pl.BlockSpec((rows, TOPK), lambda i: (0, 0)),
            pl.BlockSpec((rows, TOPK), lambda i: (0, 0)),
        ),
        scratch_shapes=[pltpu.VMEM((rows, 2 * TOPK), f32)],
        compiler_params=params(),
        name="unpack",
    )(place, kept, hid_par)


def logits_kernel(place, h0, h1, direct, swapped, h3, passed, wo, wp, to, tp, lo, lp, stats, hid):
    step = pl.program_id(0)
    odd = place[1] & 1
    hid[0:ROWS, :] = h0[...]
    hid[ROWS : 2 * ROWS, :] = h1[...]
    hid[pl.ds(pl.multiple_of(2 * ROWS + odd * HALF, HALF), HALF), :] = direct[...]
    hid[pl.ds(pl.multiple_of(2 * ROWS + (1 - odd) * HALF, HALF), HALF), :] = swapped[...]
    hid[3 * ROWS : TOK, :] = h3[...]
    hid[TOK:, :] = jnp.zeros((NY * CAP, hid.shape[1]), bf16)
    hid[TOK:, : 4 * TOPK] = passed[...]
    h = hid[0:TOK, :]
    dims = (((1,), (1,)), ((), ()))
    a = lax.dot_general(wo[...], h, dims, preferred_element_type=f32)
    b = lax.dot_general(wp[...], h, dims, preferred_element_type=f32)

    @pl.when(step == 0)
    def _():
        lo[...] = a
        lp[...] = b

    @pl.when(step > 0)
    def _():
        lo[...] += a
        lp[...] += b

    @pl.when(step == pl.num_programs(0) - 1)
    def _():
        own, par = lo[...], lp[...]
        peak = jnp.maximum(
            jnp.max(own, axis=0, keepdims=True), jnp.max(par, axis=0, keepdims=True)
        )
        total = jnp.sum(jnp.exp(own - peak), axis=0, keepdims=True) + jnp.sum(
            jnp.exp(par - peak), axis=0, keepdims=True
        )
        cross = jnp.sum(own * to[...], axis=0, keepdims=True) + jnp.sum(
            par * tp[...], axis=0, keepdims=True
        )
        stats[...] = jnp.concatenate([peak, total, cross, jnp.zeros((5, TOK), f32)], axis=0)


def logits_of(place, blocks, passed, wo, wp, to, tp):
    steps = 2
    k = D // steps
    fixed = lambda shape: pl.BlockSpec(shape, lambda i: (0, 0))
    return pl.pallas_call(
        logits_kernel,
        grid=(steps,),
        out_shape=(
            jax.ShapeDtypeStruct((COLS, TOK), f32),
            jax.ShapeDtypeStruct((COLS, TOK), f32),
            jax.ShapeDtypeStruct((8, TOK), f32),
            jax.ShapeDtypeStruct((TOK + NY * CAP, D), bf16),
        ),
        in_specs=[pl.BlockSpec(memory_space=pltpu.SMEM)]
        + [pl.BlockSpec((b.shape[0], k), lambda i: (0, i)) for b in blocks]
        + [fixed((NY * CAP, 4 * TOPK))]
        + [pl.BlockSpec((COLS, k), lambda i: (0, i))] * 2
        + [fixed((COLS, TOK))] * 2,
        out_specs=(
            fixed((COLS, TOK)),
            fixed((COLS, TOK)),
            fixed((8, TOK)),
            pl.BlockSpec((TOK + NY * CAP, k), lambda i: (0, i)),
        ),
        compiler_params=params(),
        cost_estimate=cost(2 * TOK * D * COLS * 2, 14_000_000),
        name="logits",
    )(place, *blocks, passed, wo, wp, to, tp)


def merge(parts):
    peak = parts[0][0:1]
    for p in parts[1:]:
        peak = jnp.maximum(peak, p[0:1])
    total = sum(p[1:2] * jnp.exp(p[0:1] - peak) for p in parts)
    cross = sum(p[2:3] for p in parts)
    return peak, total, cross


def merge_kernel(shifts, *refs):
    parts = []
    for ref, shift in zip(refs[:-1], shifts):
        part = ref[...]
        if shift:
            part = pltpu.roll(part, TOK - shift * ROWS, 1)
        parts.append(part)
    peak, total, cross = merge(parts)
    refs[-1][...] = jnp.concatenate([peak, total, cross, jnp.zeros((5, TOK), f32)], axis=0)


def merged(parts, shifts):
    return pl.pallas_call(
        functools.partial(merge_kernel, shifts),
        out_shape=jax.ShapeDtypeStruct((8, TOK), f32),
        in_specs=[whole()] * len(parts),
        out_specs=whole(),
        compiler_params=params(),
        name="merge",
    )(*parts)


def row_block(peak, total, cross):
    return jnp.concatenate([peak, total, cross, jnp.zeros((5, TOK), f32)], axis=0)


def ring_kernel(before, here, after, three, two):
    b, h, a = before[...], here[...], after[...]
    three[...] = row_block(*merge([b, h, a]))
    two[...] = row_block(*merge([h, a]))


def ring_merged(before, here, after):
    return pl.pallas_call(
        ring_kernel,
        out_shape=[jax.ShapeDtypeStruct((8, TOK), f32)] * 2,
        in_specs=[whole()] * 3,
        out_specs=[whole()] * 2,
        compiler_params=params(),
        name="ring_merge",
    )(before, here, after)


def final_kernel(tk, *refs):
    peak, total, cross = merge([ref[...] for ref in refs[:-1]])
    norm = peak + jnp.log(total)
    refs[-1][...] = jnp.concatenate(
        [norm, tk[...] + norm - cross, jnp.zeros((6, TOK), f32)], axis=0
    )


def final_norm(tk, parts):
    return pl.pallas_call(
        final_kernel,
        out_shape=jax.ShapeDtypeStruct((8, TOK), f32),
        in_specs=[whole()] * (len(parts) + 1),
        out_specs=whole(),
        compiler_params=params(),
        name="norm",
    )(tk, *parts)


def gradient_kernel(lo, lp, to, tp, norm, go, gp, g_own, g_par):
    n = norm[0:1, :]
    own = (loss_scale * (jnp.exp(lo[...] - n) - to[...])).astype(bf16)
    par = (loss_scale * (jnp.exp(lp[...] - n) - tp[...])).astype(bf16)
    go[...] = own
    gp[...] = par
    g_own[...] = own.T
    g_par[...] = par.T


def gradient_of(lo, lp, to, tp, norm):
    return pl.pallas_call(
        gradient_kernel,
        out_shape=[jax.ShapeDtypeStruct((COLS, TOK), bf16)] * 2
        + [jax.ShapeDtypeStruct((TOK, COLS), bf16)] * 2,
        in_specs=[whole()] * 5,
        out_specs=[whole()] * 4,
        compiler_params=params(),
        cost_estimate=cost(0, 4_000_000),
        name="gradient",
    )(lo, lp, to, tp, norm)


def terms_kernel(place, g_own, g_par, wo, wp, *rest):
    outs_a, outs_b = rest[0:4], rest[4:8]
    x = place[1]

    def features(ref, e):
        return jnp.concatenate(
            [
                ref[:, pl.ds(pl.multiple_of((e * NX + ((x + d) & (NX - 1))) * 128, 128), 128)]
                for d in range(NX)
            ],
            axis=1,
        )

    for e in range(ZSTEP):
        out = jnp.dot(g_own[...], features(wo, e), preferred_element_type=f32)
        out = out + jnp.dot(g_par[...], features(wp, e), preferred_element_type=f32)
        at = slice(e * 128, (e + 1) * 128)
        for d in range(NX):
            for r in range(NY):
                piece = out[r * ROWS : (r + 1) * ROWS, d * 128 : (d + 1) * 128]
                outs_a[d][r, :, at] = piece[:HALF].astype(outs_a[d].dtype)
                outs_b[r][d, :, at] = piece[HALF:].astype(outs_b[r].dtype)


def terms_of(place, g_own, g_par, wo, wp):
    wide = pl.BlockSpec((COLS, ZSTEP * NX * 128), lambda e, place: (0, e))
    piece = pl.BlockSpec((4, HALF, ZSTEP * 128), lambda e, place: (0, 0, e))
    out = [jax.ShapeDtypeStruct((4, HALF, NZ * 128), t) for t in (f32, bf16, bf16, bf16)]
    return pl.pallas_call(
        terms_kernel,
        grid_spec=pltpu.PrefetchScalarGridSpec(
            num_scalar_prefetch=1,
            grid=(NZ // ZSTEP,),
            in_specs=[pl.BlockSpec((TOK, COLS), lambda e, place: (0, 0))] * 2 + [wide, wide],
            out_specs=[piece] * 8,
        ),
        out_shape=out + out,
        compiler_params=params(),
        cost_estimate=cost(2 * TOK * D * COLS * 2, 16_000_000),
        name="terms",
    )(place, g_own, g_par, wo, wp)


def sum_first_kernel(*refs):
    for half in range(2):
        ins, outs = refs[4 * half : 4 * half + 4], refs[8 + 4 * half : 12 + 4 * half]
        for r in range(4):
            total = ins[0][r]
            for ref in ins[1:]:
                total = total + ref[r].astype(f32)
            outs[r][...] = total


def sum_first(a, b):
    out = jax.ShapeDtypeStruct((HALF, NZ * 128), f32)
    res = pl.pallas_call(
        sum_first_kernel,
        out_shape=[out] * 8,
        in_specs=[whole()] * 8,
        out_specs=[whole()] * 8,
        compiler_params=params(),
        name="sum_first",
    )(*a, *b)
    return res[:4], res[4:]


def sum_second_kernel(place, *refs):
    ins_a, ins_b, outs = refs[0:4], refs[4:8], refs[8:]
    spots = ((0, 0), (1, 0), (3, 0), (3, 1), (3, 2), (4, 0), (4, 1), (2, 0))
    for e in range(NZ):
        at = pl.ds(pl.multiple_of(((place[0] + e) & (NZ - 1)) * 128, 128), 128)
        k, i = spots[e]
        outs[k][i, :HALF] = ins_a[0][:, at] + ins_a[1][:, at] + ins_a[2][:, at] + ins_a[3][:, at]
        outs[k][i, HALF:] = ins_b[0][:, at] + ins_b[1][:, at] + ins_b[2][:, at] + ins_b[3][:, at]


def sum_second(place, a, b):
    return pl.pallas_call(
        sum_second_kernel,
        out_shape=[jax.ShapeDtypeStruct((n, ROWS, 128), f32) for n in (1, 1, 1, 3, 2)],
        in_specs=[pl.BlockSpec(memory_space=pltpu.SMEM)] + [whole()] * 8,
        out_specs=[whole()] * 5,
        compiler_params=params(),
        name="sum_second",
    )(place, *a, *b)


def sum_third_kernel(own, ahead, behind, three, two, out_own, out_ahead, out_behind):
    out_own[...] = own[...] + three[1:2] + two[0:1]
    out_ahead[...] = ahead[...] + three[2:3] + two[1:2]
    out_behind[...] = behind[...] + three[0:1]


def sum_third(*values):
    return pl.pallas_call(
        sum_third_kernel,
        out_shape=[jax.ShapeDtypeStruct((1, ROWS, 128), f32)] * 3,
        in_specs=[whole()] * 5,
        out_specs=[whole()] * 3,
        compiler_params=params(),
        name="sum_third",
    )(*values)


def head_kernel(g0, g1, h0, h1, out):
    total = jnp.dot(g0[...], h0[...], preferred_element_type=f32)
    total = total + jnp.dot(g1[...], h1[...], preferred_element_type=f32)
    out[...] = total.astype(bf16)


def head_grad(g0, g1, h0, h1):
    width = 1024
    return pl.pallas_call(
        head_kernel,
        grid=(D // width,),
        out_shape=jax.ShapeDtypeStruct((COLS, D), bf16),
        in_specs=[pl.BlockSpec((COLS, TOK), lambda i: (0, 0))] * 2
        + [pl.BlockSpec((TOK, width), lambda i: (0, i))] * 2,
        out_specs=pl.BlockSpec((COLS, width), lambda i: (0, i)),
        compiler_params=params(),
        cost_estimate=cost(4 * TOK * D * COLS, 10_000_000),
        name="head_grad",
    )(g0, g1, h0, h1)


def tied(*values):
    return lax.optimization_barrier(values)


def body(hidden, head_weight, teacher_ids, teacher_logits, labels, store_ids, store_logits, owner):
    y, c, z, x = (lax.axis_index(name).astype(jnp.int32) for name in AXES)
    place = jnp.stack([z, x, y, c])
    start = jnp.stack([index_of(y, c, z, x) * COLS, index_of(y, c + 1, z, x) * COLS])
    w_own = jnp.transpose(head_weight)

    packs = packs_of(
        place, owner[:, 0], teacher_ids, teacher_logits, labels[None, :], store_ids, store_logits
    )
    half = lax.dynamic_slice_in_dim(hidden, (x % 2) * HALF, HALF, 0)
    direct = send(half, dy=2)
    packs = [send(p, dy=d) if d else p for d, p in enumerate(packs)]
    *packs, direct, nearby = tied(*packs, direct, hidden)
    swapped = swap_x(direct)
    blocks = [hidden, send(nearby, dy=1), direct, swapped, send(nearby, dy=3)]
    w_par = send(w_own, dc=1)
    to, tp, tk, kept, passed = target_of(start, packs)
    lo, lp, stats, hid = logits_of(place, blocks, passed, w_own, w_par, to, tp)

    parts = [stats] + [send(stats, dx=d) for d in range(1, NX)]
    stats = merged(parts, (0,) * NX)
    parts = [stats] + [send(stats, dy=-d) for d in range(1, NY)]
    stats = merged(parts, tuple(range(NY)))
    hid_par = send(hid, dc=1)
    three, two = ring_merged(send(stats, dz=1), stats, send(stats, dz=-1))
    norm = final_norm(tk, [three, send(three, dz=-3), send(two, dz=3)])
    norm, hid_par = tied(norm, hid_par)
    next_ids, next_logits = unpacked(place, kept, hid_par)
    token_loss = norm[1, :ROWS]

    go, gp, g_own, g_par = gradient_of(lo, lp, to, tp, norm)
    g_other = send(gp, dc=1)
    terms = list(terms_of(place, g_own, g_par, w_own, w_par))
    terms[1], g_other = tied(terms[1], g_other)
    a, b = terms[0:4], terms[4:8]
    a = [a[0]] + [send(a[d], dx=d) for d in range(1, NX)]
    b = [b[0]] + [send(b[d], dy=-d) for d in range(1, NY)]
    grad_head = head_grad(go, g_other, hid, hid_par)
    *received, grad_head, next_ids, next_logits = tied(
        *a[1:], *b[1:], grad_head, next_ids, next_logits
    )
    a, b = sum_first([a[0]] + received[0:3], [b[0]] + received[3:6])
    grad_head = jnp.transpose(grad_head)
    a = [a[0]] + [send(a[d], dy=-d) for d in range(1, NY)]
    b = [b[0]] + [send(b[d], dx=d) for d in range(1, NX)]
    own, ahead, behind, three, two = sum_second(place, a, b)
    own, ahead, behind = sum_third(own, ahead, behind, send(three, dz=3), send(two, dz=-3))
    grad_hidden = own + send(ahead, dz=1) + send(behind, dz=-1)
    grad_hidden = grad_hidden.reshape(ROWS, 128).astype(bf16)
    return (grad_head, grad_hidden, token_loss, next_ids, next_logits)


def solution(mesh):
    fine = jax.sharding.Mesh(mesh.devices.reshape(NY, NC, NZ, NX), AXES)
    dp, vocab, both = ("y", "c"), ("z", "x"), AXES
    return jax.shard_map(
        body,
        mesh=fine,
        in_specs=(
            P(dp, None),
            P(None, both),
            P(dp, None),
            P(dp, None),
            P(dp),
            P(both, None),
            P(both, None),
            P(both, None),
        ),
        out_specs=(
            P(None, both),
            P(dp, vocab),
            P(dp),
            P(both, None),
            P(both, None),
        ),
        check_vma=False,
    )
```

profile of v0, /device:TPU:2, one launch (start us, length us, event | category | flops | bytes accessed | tf_op | source)
XLA Modules:
  0.0 129.3 jit_solution(8369766538017559996)
XLA Ops:
  0.8 1.0 constant_dynamic-slice_fusion
  1.7 3.3 %collective-permute-start.3 = (bf16[32,4096]{1,0:T(8,128)(2,1)S(1)}, bf16[32,4096]{1,0:T(8,128)(2,1)S(1)}, u32[]{:S(2)}, u32[]{:S(2)}) collective-permute-start(bf16[32,4096]{1,0:T(8,128)(2,1)S(1)} %constant_dynamic-slice_fusion), channel_id=1, source_target_pairs={{0,128},{1,129},{2,130},{3,131},{4,132},{5,133},{6,134},{7,135},{8... | collective-permute-start | bytes 786440 | tf_op jit(solution)/shard_map/ppermute | solution.py:40
  5.0 0.7 pad_add_fusion.place
  5.7 2.3 %pack.1 = (f32[80,128]{1,0:T(8,128)}, f32[80,128]{1,0:T(8,128)}, f32[80,128]{1,0:T(8,128)}, f32[80,128]{1,0:T(8,128)}) custom-call(s32[4]{0:T(128)} %pad_add_fusion.place, s32[16]{0:T(128)} %bitcast.18, s32[64,64]{1,0:T(8,128)} %ids.1, bf16[64,64]{1,0:T(8,128)(2,1)} %scores.1, s32[1,64]{1,0:T(1,128)} %bitcast.19, s32[16,64]{1,0:T(8,128)} %store_ids.1, ...), custom_call_target="tpu_custom_call" | custom-call | tf_op jit(solution)/shard_map/pack/pallas_call | solution.py:98
  7.9 0.7 collective-permute-start
  8.6 1.8 %collective-permute-start.1 = (f32[80,128]{1,0:T(8,128)}, f32[80,128]{1,0:T(8,128)S(1)}, u32[]{:S(2)}, u32[]{:S(2)}) collective-permute-start(f32[80,128]{1,0:T(8,128)} %get-tuple-element.71), channel_id=1, source_target_pairs={{0,128},{1,129},{2,130},{3,131},{4,132},{5,133},{6,134},{7,135},{8... | collective-permute-start | bytes 122888 | tf_op jit(solution)/shard_map/ppermute | solution.py:40
  10.4 0.9 collective-permute-start.2
  11.3 2.4 %collective-permute-done.p1 = f32[80,128]{1,0:T(8,128)S(1)} collective-permute-done((f32[80,128]{1,0:T(8,128)}, f32[80,128]{1,0:T(8,128)S(1)}, u32[]{:S(2)}, u32[]{:S(2)}) %collective-permute-start) | collective-permute-done | bytes 40992 | tf_op jit(solution)/shard_map/ppermute | solution.py:40
  13.8 0.6 collective-permute-done.1.p2
  14.3 0.3 collective-permute-done.2.p3
  14.7 2.6 %collective-permute-start.6 = (bf16[64,4096]{1,0:T(8,128)(2,1)}, bf16[64,4096]{1,0:T(8,128)(2,1)S(1)}, u32[]{:S(2)}, u32[]{:S(2)}) collective-permute-start(bf16[64,4096]{1,0:T(8,128)(2,1)} %h0.1), channel_id=1, source_target_pairs={{0,192},{1,193},{2,194},{3,195},{4,196},{5,197},{6,198},{7,199},{8... | collective-permute-start | bytes 1572872 | tf_op jit(solution)/shard_map/ppermute | solution.py:40
  17.2 1.4 %collective-permute-start.5 = (bf16[32,4096]{1,0:T(8,128)(2,1)S(1)}, bf16[32,4096]{1,0:T(8,128)(2,1)S(1)}, u32[]{:S(2)}, u32[]{:S(2)}) collective-permute-start(bf16[32,4096]{1,0:T(8,128)(2,1)S(1)} %collective-permute-done.3.direct), channel_id=1, source_target_pairs={{0,1},{1,0},{2,3},{3,2},{4,5},{5,4},{6,7},{7,6},{8,9},{9,8},{10,11... | collective-permute-start | bytes 786440 | tf_op jit(solution)/shard_map/ppermute | solution.py:51
  18.7 0.8 copy-done.2
  19.4 10.7 %target.1 = (f32[592,256]{1,0:T(8,128)S(1)}, f32[592,256]{1,0:T(8,128)S(1)}, f32[1,256]{1,0:T(1,128)S(1)}, f32[16,128]{1,0:T(8,128)S(1)}, bf16[16,256]{1,0:T(8,128)(2,1)S(1)}) custom-call(s32[2]{0:T(128)S(1)} %pad_add_fusion.1.start_ref, f32[80,128]{1,0:T(8,128)S(1)} %copy-done.2, f32[80,128]{1,0:T(8,128)S(1)} %collective-permute-done.p1, ...), custom_call_target="tpu_custom_call" | custom-call | flops 1000000 | bytes 1400000 | tf_op jit(solution)/shard_map/target/pallas_call | solution.py:148
  30.1 0.8 collective-permute-done.4.h1
  30.9 1.0 copy-done.1
  32.0 0.7 copy-done.3
  32.7 7.2 %logits.1 = (f32[592,256]{1,0:T(8,128)S(1)}, f32[592,256]{1,0:T(8,128)S(1)}, f32[8,256]{1,0:T(8,128)S(1)}, bf16[272,4096]{1,0:T(8,128)(2,1)}) custom-call(s32[4]{0:T(128)S(1)} %copy-done.3, bf16[64,4096]{1,0:T(8,128)(2,1)S(1)} %copy-done.1, bf16[64,4096]{1,0:T(8,128)(2,1)S(1)} %collective-permute-done.4.h1, ...), custom_call_target="tpu_custom_call" | custom-call | flops 2483027968 | bytes 14000000 | tf_op jit(solution)/shard_map/logits/pallas_call | solution.py:249
  39.8 1.6 %collective-permute-start.10 = (f32[8,256]{1,0:T(8,128)S(1)}, f32[8,256]{1,0:T(8,128)S(1)}, u32[]{:S(2)}, u32[]{:S(2)}) collective-permute-start(f32[8,256]{1,0:T(8,128)S(1)} %get-tuple-element.85.refs_0_), channel_id=1, source_target_pairs={{0,3},{1,0},{2,1},{3,2},{4,7},{5,4},{6,5},{7,6},{8,11},{9,8},{10,9... | collective-permute-start | bytes 24584 | tf_op jit(solution)/shard_map/ppermute | solution.py:40
  41.4 1.4 %collective-permute-start.9 = (f32[8,256]{1,0:T(8,128)S(1)}, f32[8,256]{1,0:T(8,128)S(1)}, u32[]{:S(2)}, u32[]{:S(2)}) collective-permute-start(f32[8,256]{1,0:T(8,128)S(1)} %get-tuple-element.85.refs_0_), channel_id=1, source_target_pairs={{0,2},{1,3},{2,0},{3,1},{4,6},{5,7},{6,4},{7,5},{8,10},{9,11},{10,... | collective-permute-start | bytes 24584 | tf_op jit(solution)/shard_map/ppermute | solution.py:40
  42.8 1.8 %collective-permute-start.8 = (f32[8,256]{1,0:T(8,128)S(1)}, f32[8,256]{1,0:T(8,128)S(1)}, u32[]{:S(2)}, u32[]{:S(2)}) collective-permute-start(f32[8,256]{1,0:T(8,128)S(1)} %get-tuple-element.85.refs_0_), channel_id=1, source_target_pairs={{0,1},{1,2},{2,3},{3,0},{4,5},{5,6},{6,7},{7,4},{8,9},{9,10},{10,1... | collective-permute-start | bytes 24584 | tf_op jit(solution)/shard_map/ppermute | solution.py:40
  44.6 1.9 %collective-permute-done.9.refs_2_ = f32[8,256]{1,0:T(8,128)S(1)} collective-permute-done((f32[8,256]{1,0:T(8,128)S(1)}, f32[8,256]{1,0:T(8,128)S(1)}, u32[]{:S(2)}, u32[]{:S(2)}) %collective-permute-start.9) | collective-permute-done | bytes 8224 | tf_op jit(solution)/shard_map/ppermute | solution.py:40
  46.7 3.6 %collective-permute-start.12 = (f32[8,256]{1,0:T(8,128)S(1)}, f32[8,256]{1,0:T(8,128)S(1)}, u32[]{:S(2)}, u32[]{:S(2)}) collective-permute-start(f32[8,256]{1,0:T(8,128)S(1)} %merge.2.refs_0_), channel_id=1, source_target_pairs={{0,128},{1,129},{2,130},{3,131},{4,132},{5,133},{6,134},{7,135},{8... | collective-permute-start | bytes 24584 | tf_op jit(solution)/shard_map/ppermute | solution.py:40
  50.3 1.2 collective-permute-done.13.refs_3_
  51.5 0.6 collective-permute-done.12.refs_2_
  52.1 1.8 %collective-permute-done.11.refs_1_ = f32[8,256]{1,0:T(8,128)S(1)} collective-permute-done((f32[8,256]{1,0:T(8,128)S(1)}, f32[8,256]{1,0:T(8,128)S(1)}, u32[]{:S(2)}, u32[]{:S(2)}) %collective-permute-start.11) | collective-permute-done | bytes 8224 | tf_op jit(solution)/shard_map/ppermute | solution.py:40
  54.0 5.9 %collective-permute-start.15 = (f32[8,256]{1,0:T(8,128)S(1)}, f32[8,256]{1,0:T(8,128)S(1)}, u32[]{:S(2)}, u32[]{:S(2)}) collective-permute-start(f32[8,256]{1,0:T(8,128)S(1)} %merge.3.here), channel_id=1, source_target_pairs={{0,28},{1,29},{2,30},{3,31},{4,0},{5,1},{6,2},{7,3},{8,4},{9,5},{1... | collective-permute-start | bytes 24584 | tf_op jit(solution)/shard_map/ppermute | solution.py:40
  59.9 1.4 %collective-permute-done.15.after = f32[8,256]{1,0:T(8,128)S(1)} collective-permute-done((f32[8,256]{1,0:T(8,128)S(1)}, f32[8,256]{1,0:T(8,128)S(1)}, u32[]{:S(2)}, u32[]{:S(2)}) %collective-permute-start.15) | collective-permute-done | bytes 8224 | tf_op jit(solution)/shard_map/ppermute | solution.py:40
  61.3 3.5 %collective-permute-done.14.before = f32[8,256]{1,0:T(8,128)S(1)} collective-permute-done((f32[8,256]{1,0:T(8,128)S(1)}, f32[8,256]{1,0:T(8,128)S(1)}, u32[]{:S(2)}, u32[]{:S(2)}) %collective-permute-start.14) | collective-permute-done | bytes 8224 | tf_op jit(solution)/shard_map/ppermute | solution.py:40
  64.9 5.0 %collective-permute-start.16 = (f32[8,256]{1,0:T(8,128)S(1)}, f32[8,256]{1,0:T(8,128)S(1)}, u32[]{:S(2)}, u32[]{:S(2)}) collective-permute-start(f32[8,256]{1,0:T(8,128)S(1)} %get-tuple-element.86.refs_0_), channel_id=1, source_target_pairs={{0,20},{1,21},{2,22},{3,23},{4,24},{5,25},{6,26},{7,27},{8,28},{9,... | collective-permute-start | bytes 24584 | tf_op jit(solution)/shard_map/ppermute | solution.py:40
  69.9 1.6 %collective-permute-done.17.refs_2_ = f32[8,256]{1,0:T(8,128)S(1)} collective-permute-done((f32[8,256]{1,0:T(8,128)S(1)}, f32[8,256]{1,0:T(8,128)S(1)}, u32[]{:S(2)}, u32[]{:S(2)}) %collective-permute-start.17) | collective-permute-done | bytes 8224 | tf_op jit(solution)/shard_map/ppermute | solution.py:40
  71.6 0.3 gradient.1
  72.1 7.2 %terms.1 = (f32[4,32,1024]{2,1,0:T(8,128)S(1)}, bf16[4,32,1024]{2,1,0:T(8,128)(2,1)S(1)}, bf16[4,32,1024]{2,1,0:T(8,128)(2,1)S(1)}, bf16[4,32,1024]{2,1,0:T(8,12...) custom-call(s32[4]{0:T(128)S(1)} %copy-done.4, ...), custom_call_target="tpu_custom_call" | custom-call | flops 2483027968 | bytes 16000000 | tf_op jit(solution)/shard_map/terms/pallas_call | solution.py:397
  79.3 1.6 %collective-permute-start.21 = (bf16[4,32,1024]{2,1,0:T(8,128)(2,1)S(1)}, bf16[4,32,1024]{2,1,0:T(8,128)(2,1)S(1)}, u32[]{:S(2)}, u32[]{:S(2)}) collective-permute-start(bf16[4,32,1024]{2,1,0:T(8,128)(2,1)S(1)} %get-tuple-element.95), channel_id=1, source_target_pairs={{0,2},{1,3},{2,0},{3,1},{4,6},{5,7},{6,4},{7,5},{8,10},{9,11},{10,... | collective-permute-start | bytes 786440 | tf_op jit(solution)/shard_map/ppermute | solution.py:40
  80.9 2.0 %collective-permute-start.22 = (bf16[4,32,1024]{2,1,0:T(8,128)(2,1)S(1)}, bf16[4,32,1024]{2,1,0:T(8,128)(2,1)S(1)}, u32[]{:S(2)}, u32[]{:S(2)}) collective-permute-start(bf16[4,32,1024]{2,1,0:T(8,128)(2,1)S(1)} %get-tuple-element.96), channel_id=1, source_target_pairs={{0,3},{1,0},{2,1},{3,2},{4,7},{5,4},{6,5},{7,6},{8,11},{9,8},{10,9... | collective-permute-start | bytes 786440 | tf_op jit(solution)/shard_map/ppermute | solution.py:40
  82.9 1.4 %collective-permute-start.23 = (bf16[4,32,1024]{2,1,0:T(8,128)(2,1)S(1)}, bf16[4,32,1024]{2,1,0:T(8,128)(2,1)S(1)}, u32[]{:S(2)}, u32[]{:S(2)}) collective-permute-start(bf16[4,32,1024]{2,1,0:T(8,128)(2,1)S(1)} %get-tuple-element.97), channel_id=1, source_target_pairs={{0,192},{1,193},{2,194},{3,195},{4,196},{5,197},{6,198},{7,199},{8... | collective-permute-start | bytes 786440 | tf_op jit(solution)/shard_map/ppermute | solution.py:40
  84.3 1.4 %collective-permute-start.24 = (bf16[4,32,1024]{2,1,0:T(8,128)(2,1)S(1)}, bf16[4,32,1024]{2,1,0:T(8,128)(2,1)S(1)}, u32[]{:S(2)}, u32[]{:S(2)}) collective-permute-start(bf16[4,32,1024]{2,1,0:T(8,128)(2,1)S(1)} %get-tuple-element.98), channel_id=1, source_target_pairs={{0,128},{1,129},{2,130},{3,131},{4,132},{5,133},{6,134},{7,135},{8... | collective-permute-start | bytes 786440 | tf_op jit(solution)/shard_map/ppermute | solution.py:40
  85.7 0.1 collective-permute-start.25
  85.9 4.2 %collective-permute-done.21.refs_2_ = bf16[4,32,1024]{2,1,0:T(8,128)(2,1)S(1)} collective-permute-done((bf16[4,32,1024]{2,1,0:T(8,128)(2,1)S(1)}, bf16[4,32,1024]{2,1,0:T(8,128)(2,1)S(1)}, u32[]{:S(2)}, u32[]{:S(2)}) %collective-permute-start.21) | collective-permute-done | bytes 262176 | tf_op jit(solution)/shard_map/ppermute | solution.py:40
  90.1 1.0 collective-permute-start.20
  91.1 1.4 %unpack.1 = (s32[32,64]{1,0:T(8,128)}, bf16[32,64]{1,0:T(8,128)(2,1)}) custom-call(s32[4]{0:T(128)S(1)} %copy-done.4, f32[16,128]{1,0:T(8,128)S(1)} %get-tuple-element.103.kept, bf16[272,4096]{1,0:T(8,128)(2,1)S(1)} %collective-permute-done.18.h1.digits), custom_call_target="tpu_custom_call" | custom-call | tf_op jit(solution)/shard_map/unpack/pallas_call | solution.py:183
  92.4 4.7 %head_grad.1 = bf16[592,4096]{1,0:T(8,128)(2,1)} custom-call(bf16[592,256]{1,0:T(8,128)(2,1)S(1)} %get-tuple-element.100.g0, bf16[592,256]{1,0:T(8,128)(2,1)S(1)} %collective-permute-done.19.g1, bf16[272,4096]{1,0:T(8,128)(2,1)S(1)} %copy-done, bf16[272,4096]{1,0:T(8,128)(2,1)S(1)} %collective-permute-done.18.h1.digits), custom_call_target="tpu_custom_call" | custom-call | flops 2483027968 | bytes 10000000 | tf_op jit(solution)/shard_map/head_grad/pallas_call | solution.py:481
  97.1 2.2 %collective-permute-done.25.refs_7_ = bf16[4,32,1024]{2,1,0:T(8,128)(2,1)S(1)} collective-permute-done((bf16[4,32,1024]{2,1,0:T(8,128)(2,1)S(1)}, bf16[4,32,1024]{2,1,0:T(8,128)(2,1)S(1)}, u32[]{:S(2)}, u32[]{:S(2)}) %collective-permute-start.25) | collective-permute-done | bytes 262176 | tf_op jit(solution)/shard_map/ppermute | solution.py:40
  99.3 0.2 sum_first.1
  99.5 0.9 collective-permute-start.26
  100.4 1.4 %collective-permute-start.27 = (f32[32,1024]{1,0:T(8,128)S(1)}, f32[32,1024]{1,0:T(8,128)S(1)}, u32[]{:S(2)}, u32[]{:S(2)}) collective-permute-start(f32[32,1024]{1,0:T(8,128)S(1)} %get-tuple-element.117), channel_id=1, source_target_pairs={{0,128},{1,129},{2,130},{3,131},{4,132},{5,133},{6,134},{7,135},{8... | collective-permute-start | bytes 393224 | tf_op jit(solution)/shard_map/ppermute | solution.py:40
  101.9 0.8 collective-permute-start.28
  102.7 0.2 collective-permute-start.29
  102.9 3.3 %collective-permute-start.30 = (f32[32,1024]{1,0:T(8,128)S(1)}, f32[32,1024]{1,0:T(8,128)S(1)}, u32[]{:S(2)}, u32[]{:S(2)}) collective-permute-start(f32[32,1024]{1,0:T(8,128)S(1)} %get-tuple-element.121), channel_id=1, source_target_pairs={{0,2},{1,3},{2,0},{3,1},{4,6},{5,7},{6,4},{7,5},{8,10},{9,11},{10,... | collective-permute-start | bytes 393224 | tf_op jit(solution)/shard_map/ppermute | solution.py:40
  106.2 1.4 %collective-permute-start.31 = (f32[32,1024]{1,0:T(8,128)S(1)}, f32[32,1024]{1,0:T(8,128)S(1)}, u32[]{:S(2)}, u32[]{:S(2)}) collective-permute-start(f32[32,1024]{1,0:T(8,128)S(1)} %get-tuple-element.122), channel_id=1, source_target_pairs={{0,3},{1,0},{2,1},{3,2},{4,7},{5,4},{6,5},{7,6},{8,11},{9,8},{10,9... | collective-permute-start | bytes 393224 | tf_op jit(solution)/shard_map/ppermute | solution.py:40
  107.6 0.3 collective-permute-done.27.refs_2_
  107.9 1.8 %collective-permute-done.28.refs_3_ = f32[32,1024]{1,0:T(8,128)S(1)} collective-permute-done((f32[32,1024]{1,0:T(8,128)S(1)}, f32[32,1024]{1,0:T(8,128)S(1)}, u32[]{:S(2)}, u32[]{:S(2)}) %collective-permute-start.28) | collective-permute-done | bytes 131104 | tf_op jit(solution)/shard_map/ppermute | solution.py:40
  109.7 0.5 collective-permute-done.30.refs_6_
  110.2 1.4 %collective-permute-done.31.refs_7_ = f32[32,1024]{1,0:T(8,128)S(1)} collective-permute-done((f32[32,1024]{1,0:T(8,128)S(1)}, f32[32,1024]{1,0:T(8,128)S(1)}, u32[]{:S(2)}, u32[]{:S(2)}) %collective-permute-start.31) | collective-permute-done | bytes 131104 | tf_op jit(solution)/shard_map/ppermute | solution.py:40
  111.6 0.7 sum_second.1
  112.3 2.7 %collective-permute-start.32 = (f32[3,64,128]{2,1,0:T(8,128)S(1)}, f32[3,64,128]{2,1,0:T(8,128)S(1)}, u32[]{:S(2)}, u32[]{:S(2)}) collective-permute-start(f32[3,64,128]{2,1,0:T(8,128)S(1)} %get-tuple-element.126), channel_id=1, source_target_pairs={{0,12},{1,13},{2,14},{3,15},{4,16},{5,17},{6,18},{7,19},{8,20},{9,... | collective-permute-start | bytes 294920 | tf_op jit(solution)/shard_map/ppermute | solution.py:40
  114.9 2.5 %collective-permute-start.33 = (f32[2,64,128]{2,1,0:T(8,128)S(1)}, f32[2,64,128]{2,1,0:T(8,128)S(1)}, u32[]{:S(2)}, u32[]{:S(2)}) collective-permute-start(f32[2,64,128]{2,1,0:T(8,128)S(1)} %get-tuple-element.127), channel_id=1, source_target_pairs={{0,20},{1,21},{2,22},{3,23},{4,24},{5,25},{6,26},{7,27},{8,28},{9,... | collective-permute-start | bytes 196616 | tf_op jit(solution)/shard_map/ppermute | solution.py:40
  117.5 3.6 %collective-permute-done.33.two = f32[2,64,128]{2,1,0:T(8,128)S(1)} collective-permute-done((f32[2,64,128]{2,1,0:T(8,128)S(1)}, f32[2,64,128]{2,1,0:T(8,128)S(1)}, u32[]{:S(2)}, u32[]{:S(2)}) %collective-permute-start.33) | collective-permute-done | bytes 65568 | tf_op jit(solution)/shard_map/ppermute | solution.py:40
  121.0 2.1 %collective-permute-start.34 = (f32[1,64,128]{2,1,0:T(8,128)S(1)}, f32[1,64,128]{2,1,0:T(8,128)S(1)}, u32[]{:S(2)}, u32[]{:S(2)}) collective-permute-start(f32[1,64,128]{2,1,0:T(8,128)S(1)} %get-tuple-element.129), channel_id=1, source_target_pairs={{0,4},{1,5},{2,6},{3,7},{4,8},{5,9},{6,10},{7,11},{8,12},{9,13},{1... | collective-permute-start | bytes 98312 | tf_op jit(solution)/shard_map/ppermute | solution.py:40
  123.2 2.1 %collective-permute-start.35 = (f32[1,64,128]{2,1,0:T(8,128)S(1)}, f32[1,64,128]{2,1,0:T(8,128)S(1)}, u32[]{:S(2)}, u32[]{:S(2)}) collective-permute-start(f32[1,64,128]{2,1,0:T(8,128)S(1)} %get-tuple-element.130), channel_id=1, source_target_pairs={{0,28},{1,29},{2,30},{3,31},{4,0},{5,1},{6,2},{7,3},{8,4},{9,5},{1... | collective-permute-start | bytes 98312 | tf_op jit(solution)/shard_map/ppermute | solution.py:40
  125.3 0.5 slice_bitcast_fusion
  125.8 1.3 collective-permute-done.34
  127.1 1.6 %collective-permute-done.35 = f32[1,64,128]{2,1,0:T(8,128)S(1)} collective-permute-done((f32[1,64,128]{2,1,0:T(8,128)S(1)}, f32[1,64,128]{2,1,0:T(8,128)S(1)}, u32[]{:S(2)}, u32[]{:S(2)}) %collective-permute-start.35) | collective-permute-done | bytes 32800 | tf_op jit(solution)/shard_map/ppermute | solution.py:40
  128.7 0.6 fusion
  (37 shorter events, 0.7 us)
Async XLA Ops:
  0.6 30.3 %collective-permute-start.7 = (bf16[592,4096]{1,0:T(8,128)(2,1)}, bf16[592,4096]{1,0:T(8,128)(2,1)}, u32[]{:S(2)}, u32[]{:S(2)}) collective-permute-start(bf16[592,4096]{1,0:T(8,128)(2,1)} %bitcast.14), channel_id=1, source_target_pairs={{0,32},{1,33},{2,34},{3,35},{4,36},{5,37},{6,38},{7,39},{8,40},{9,... | collective-permute-start | bytes 14549000 | tf_op jit(solution)/shard_map/ppermute | solution.py:40
  1.7 12.9 %collective-permute-start.3 = (bf16[32,4096]{1,0:T(8,128)(2,1)S(1)}, bf16[32,4096]{1,0:T(8,128)(2,1)S(1)}, u32[]{:S(2)}, u32[]{:S(2)}) collective-permute-start(bf16[32,4096]{1,0:T(8,128)(2,1)S(1)} %constant_dynamic-slice_fusion), channel_id=1, source_target_pairs={{0,128},{1,129},{2,130},{3,131},{4,132},{5,133},{6,134},{7,135},{8... | collective-permute-start | bytes 786440 | tf_op jit(solution)/shard_map/ppermute | solution.py:40
  7.9 5.8 %collective-permute-start = (f32[80,128]{1,0:T(8,128)}, f32[80,128]{1,0:T(8,128)S(1)}, u32[]{:S(2)}, u32[]{:S(2)}) collective-permute-start(f32[80,128]{1,0:T(8,128)} %get-tuple-element.70), channel_id=1, source_target_pairs={{0,64},{1,65},{2,66},{3,67},{4,68},{5,69},{6,70},{7,71},{8,72},{9,... | collective-permute-start | bytes 122888 | tf_op jit(solution)/shard_map/ppermute | solution.py:40
  8.6 5.7 %collective-permute-start.1 = (f32[80,128]{1,0:T(8,128)}, f32[80,128]{1,0:T(8,128)S(1)}, u32[]{:S(2)}, u32[]{:S(2)}) collective-permute-start(f32[80,128]{1,0:T(8,128)} %get-tuple-element.71), channel_id=1, source_target_pairs={{0,128},{1,129},{2,130},{3,131},{4,132},{5,133},{6,134},{7,135},{8... | collective-permute-start | bytes 122888 | tf_op jit(solution)/shard_map/ppermute | solution.py:40
  10.4 4.2 %collective-permute-start.2 = (f32[80,128]{1,0:T(8,128)}, f32[80,128]{1,0:T(8,128)S(1)}, u32[]{:S(2)}, u32[]{:S(2)}) collective-permute-start(f32[80,128]{1,0:T(8,128)} %get-tuple-element.72), channel_id=1, source_target_pairs={{0,192},{1,193},{2,194},{3,195},{4,196},{5,197},{6,198},{7,199},{8... | collective-permute-start | bytes 122888 | tf_op jit(solution)/shard_map/ppermute | solution.py:40
  14.7 15.5 %collective-permute-start.6 = (bf16[64,4096]{1,0:T(8,128)(2,1)}, bf16[64,4096]{1,0:T(8,128)(2,1)S(1)}, u32[]{:S(2)}, u32[]{:S(2)}) collective-permute-start(bf16[64,4096]{1,0:T(8,128)(2,1)} %h0.1), channel_id=1, source_target_pairs={{0,192},{1,193},{2,194},{3,195},{4,196},{5,197},{6,198},{7,199},{8... | collective-permute-start | bytes 1572872 | tf_op jit(solution)/shard_map/ppermute | solution.py:40
  17.2 13.7 %collective-permute-start.4 = (bf16[64,4096]{1,0:T(8,128)(2,1)}, bf16[64,4096]{1,0:T(8,128)(2,1)S(1)}, u32[]{:S(2)}, u32[]{:S(2)}) collective-permute-start(bf16[64,4096]{1,0:T(8,128)(2,1)} %h0.1), channel_id=1, source_target_pairs={{0,64},{1,65},{2,66},{3,67},{4,68},{5,69},{6,70},{7,71},{8,72},{9,... | collective-permute-start | bytes 1572872 | tf_op jit(solution)/shard_map/ppermute | solution.py:40
  17.2 12.9 %collective-permute-start.5 = (bf16[32,4096]{1,0:T(8,128)(2,1)S(1)}, bf16[32,4096]{1,0:T(8,128)(2,1)S(1)}, u32[]{:S(2)}, u32[]{:S(2)}) collective-permute-start(bf16[32,4096]{1,0:T(8,128)(2,1)S(1)} %collective-permute-done.3.direct), channel_id=1, source_target_pairs={{0,1},{1,0},{2,3},{3,2},{4,5},{5,4},{6,7},{7,6},{8,9},{9,8},{10,11... | collective-permute-start | bytes 786440 | tf_op jit(solution)/shard_map/ppermute | solution.py:51
  18.7 0.8 copy-start.2
  30.9 1.0 copy-start.1
  32.0 0.7 copy-start.3
  32.7 39.4 %copy-start.4 = (s32[4]{0:T(128)S(1)}, s32[4]{0:T(128)}, u32[]{:S(2)}) copy-start(s32[4]{0:T(128)} %pad_add_fusion.place) | copy-start | bytes 52
  39.8 31.8 %collective-permute-start.18 = (bf16[272,4096]{1,0:T(8,128)(2,1)}, bf16[272,4096]{1,0:T(8,128)(2,1)S(1)}, u32[]{:S(2)}, u32[]{:S(2)}) collective-permute-start(bf16[272,4096]{1,0:T(8,128)(2,1)} %get-tuple-element.88.h0), channel_id=1, source_target_pairs={{0,32},{1,33},{2,34},{3,35},{4,36},{5,37},{6,38},{7,39},{8,40},{9,... | collective-permute-start | bytes 6684680 | tf_op jit(solution)/shard_map/ppermute | solution.py:40
  39.8 4.8 %collective-permute-start.10 = (f32[8,256]{1,0:T(8,128)S(1)}, f32[8,256]{1,0:T(8,128)S(1)}, u32[]{:S(2)}, u32[]{:S(2)}) collective-permute-start(f32[8,256]{1,0:T(8,128)S(1)} %get-tuple-element.85.refs_0_), channel_id=1, source_target_pairs={{0,3},{1,0},{2,1},{3,2},{4,7},{5,4},{6,5},{7,6},{8,11},{9,8},{10,9... | collective-permute-start | bytes 24584 | tf_op jit(solution)/shard_map/ppermute | solution.py:40
  41.4 5.2 %collective-permute-start.9 = (f32[8,256]{1,0:T(8,128)S(1)}, f32[8,256]{1,0:T(8,128)S(1)}, u32[]{:S(2)}, u32[]{:S(2)}) collective-permute-start(f32[8,256]{1,0:T(8,128)S(1)} %get-tuple-element.85.refs_0_), channel_id=1, source_target_pairs={{0,2},{1,3},{2,0},{3,1},{4,6},{5,7},{6,4},{7,5},{8,10},{9,11},{10,... | collective-permute-start | bytes 24584 | tf_op jit(solution)/shard_map/ppermute | solution.py:40
  42.8 3.8 %collective-permute-start.8 = (f32[8,256]{1,0:T(8,128)S(1)}, f32[8,256]{1,0:T(8,128)S(1)}, u32[]{:S(2)}, u32[]{:S(2)}) collective-permute-start(f32[8,256]{1,0:T(8,128)S(1)} %get-tuple-element.85.refs_0_), channel_id=1, source_target_pairs={{0,1},{1,2},{2,3},{3,0},{4,5},{5,6},{6,7},{7,4},{8,9},{9,10},{10,1... | collective-permute-start | bytes 24584 | tf_op jit(solution)/shard_map/ppermute | solution.py:40
  46.6 4.9 %collective-permute-start.13 = (f32[8,256]{1,0:T(8,128)S(1)}, f32[8,256]{1,0:T(8,128)S(1)}, u32[]{:S(2)}, u32[]{:S(2)}) collective-permute-start(f32[8,256]{1,0:T(8,128)S(1)} %merge.2.refs_0_), channel_id=1, source_target_pairs={{0,64},{1,65},{2,66},{3,67},{4,68},{5,69},{6,70},{7,71},{8,72},{9,... | collective-permute-start | bytes 24584 | tf_op jit(solution)/shard_map/ppermute | solution.py:40
  46.7 5.4 %collective-permute-start.12 = (f32[8,256]{1,0:T(8,128)S(1)}, f32[8,256]{1,0:T(8,128)S(1)}, u32[]{:S(2)}, u32[]{:S(2)}) collective-permute-start(f32[8,256]{1,0:T(8,128)S(1)} %merge.2.refs_0_), channel_id=1, source_target_pairs={{0,128},{1,129},{2,130},{3,131},{4,132},{5,133},{6,134},{7,135},{8... | collective-permute-start | bytes 24584 | tf_op jit(solution)/shard_map/ppermute | solution.py:40
  50.3 3.7 %collective-permute-start.11 = (f32[8,256]{1,0:T(8,128)S(1)}, f32[8,256]{1,0:T(8,128)S(1)}, u32[]{:S(2)}, u32[]{:S(2)}) collective-permute-start(f32[8,256]{1,0:T(8,128)S(1)} %merge.2.refs_0_), channel_id=1, source_target_pairs={{0,192},{1,193},{2,194},{3,195},{4,196},{5,197},{6,198},{7,199},{8... | collective-permute-start | bytes 24584 | tf_op jit(solution)/shard_map/ppermute | solution.py:40
  54.0 7.3 %collective-permute-start.15 = (f32[8,256]{1,0:T(8,128)S(1)}, f32[8,256]{1,0:T(8,128)S(1)}, u32[]{:S(2)}, u32[]{:S(2)}) collective-permute-start(f32[8,256]{1,0:T(8,128)S(1)} %merge.3.here), channel_id=1, source_target_pairs={{0,28},{1,29},{2,30},{3,31},{4,0},{5,1},{6,2},{7,3},{8,4},{9,5},{1... | collective-permute-start | bytes 24584 | tf_op jit(solution)/shard_map/ppermute | solution.py:40
  59.9 4.9 %collective-permute-start.14 = (f32[8,256]{1,0:T(8,128)S(1)}, f32[8,256]{1,0:T(8,128)S(1)}, u32[]{:S(2)}, u32[]{:S(2)}) collective-permute-start(f32[8,256]{1,0:T(8,128)S(1)} %merge.3.here), channel_id=1, source_target_pairs={{0,4},{1,5},{2,6},{3,7},{4,8},{5,9},{6,10},{7,11},{8,12},{9,13},{1... | collective-permute-start | bytes 24584 | tf_op jit(solution)/shard_map/ppermute | solution.py:40
  64.8 6.7 %collective-permute-start.17 = (f32[8,256]{1,0:T(8,128)S(1)}, f32[8,256]{1,0:T(8,128)S(1)}, u32[]{:S(2)}, u32[]{:S(2)}) collective-permute-start(f32[8,256]{1,0:T(8,128)S(1)} %get-tuple-element.87), channel_id=1, source_target_pairs={{0,12},{1,13},{2,14},{3,15},{4,16},{5,17},{6,18},{7,19},{8,20},{9,... | collective-permute-start | bytes 24584 | tf_op jit(solution)/shard_map/ppermute | solution.py:40
  64.9 6.6 %collective-permute-start.16 = (f32[8,256]{1,0:T(8,128)S(1)}, f32[8,256]{1,0:T(8,128)S(1)}, u32[]{:S(2)}, u32[]{:S(2)}) collective-permute-start(f32[8,256]{1,0:T(8,128)S(1)} %get-tuple-element.86.refs_0_), channel_id=1, source_target_pairs={{0,20},{1,21},{2,22},{3,23},{4,24},{5,25},{6,26},{7,27},{8,28},{9,... | collective-permute-start | bytes 24584 | tf_op jit(solution)/shard_map/ppermute | solution.py:40
  71.9 13.8 %collective-permute-start.19 = (bf16[592,256]{1,0:T(8,128)(2,1)S(1)}, bf16[592,256]{1,0:T(8,128)(2,1)S(1)}, u32[]{:S(2)}, u32[]{:S(2)}) collective-permute-start(bf16[592,256]{1,0:T(8,128)(2,1)S(1)} %get-tuple-element.93), channel_id=1, source_target_pairs={{0,32},{1,33},{2,34},{3,35},{4,36},{5,37},{6,38},{7,39},{8,40},{9,... | collective-permute-start | bytes 909320 | tf_op jit(solution)/shard_map/ppermute | solution.py:40
  72.1 20.4 %copy-start = (bf16[272,4096]{1,0:T(8,128)(2,1)S(1)}, bf16[272,4096]{1,0:T(8,128)(2,1)}, u32[]{:S(2)}) copy-start(bf16[272,4096]{1,0:T(8,128)(2,1)} %get-tuple-element.88.h0) | copy-start | bytes 6684676
  79.3 10.7 %collective-permute-start.21 = (bf16[4,32,1024]{2,1,0:T(8,128)(2,1)S(1)}, bf16[4,32,1024]{2,1,0:T(8,128)(2,1)S(1)}, u32[]{:S(2)}, u32[]{:S(2)}) collective-permute-start(bf16[4,32,1024]{2,1,0:T(8,128)(2,1)S(1)} %get-tuple-element.95), channel_id=1, source_target_pairs={{0,2},{1,3},{2,0},{3,1},{4,6},{5,7},{6,4},{7,5},{8,10},{9,11},{10,... | collective-permute-start | bytes 786440 | tf_op jit(solution)/shard_map/ppermute | solution.py:40
  80.9 16.2 %collective-permute-start.22 = (bf16[4,32,1024]{2,1,0:T(8,128)(2,1)S(1)}, bf16[4,32,1024]{2,1,0:T(8,128)(2,1)S(1)}, u32[]{:S(2)}, u32[]{:S(2)}) collective-permute-start(bf16[4,32,1024]{2,1,0:T(8,128)(2,1)S(1)} %get-tuple-element.96), channel_id=1, source_target_pairs={{0,3},{1,0},{2,1},{3,2},{4,7},{5,4},{6,5},{7,6},{8,11},{9,8},{10,9... | collective-permute-start | bytes 786440 | tf_op jit(solution)/shard_map/ppermute | solution.py:40
  82.9 14.2 %collective-permute-start.23 = (bf16[4,32,1024]{2,1,0:T(8,128)(2,1)S(1)}, bf16[4,32,1024]{2,1,0:T(8,128)(2,1)S(1)}, u32[]{:S(2)}, u32[]{:S(2)}) collective-permute-start(bf16[4,32,1024]{2,1,0:T(8,128)(2,1)S(1)} %get-tuple-element.97), channel_id=1, source_target_pairs={{0,192},{1,193},{2,194},{3,195},{4,196},{5,197},{6,198},{7,199},{8... | collective-permute-start | bytes 786440 | tf_op jit(solution)/shard_map/ppermute | solution.py:40
  84.3 12.8 %collective-permute-start.24 = (bf16[4,32,1024]{2,1,0:T(8,128)(2,1)S(1)}, bf16[4,32,1024]{2,1,0:T(8,128)(2,1)S(1)}, u32[]{:S(2)}, u32[]{:S(2)}) collective-permute-start(bf16[4,32,1024]{2,1,0:T(8,128)(2,1)S(1)} %get-tuple-element.98), channel_id=1, source_target_pairs={{0,128},{1,129},{2,130},{3,131},{4,132},{5,133},{6,134},{7,135},{8... | collective-permute-start | bytes 786440 | tf_op jit(solution)/shard_map/ppermute | solution.py:40
  85.7 13.6 %collective-permute-start.25 = (bf16[4,32,1024]{2,1,0:T(8,128)(2,1)S(1)}, bf16[4,32,1024]{2,1,0:T(8,128)(2,1)S(1)}, u32[]{:S(2)}, u32[]{:S(2)}) collective-permute-start(bf16[4,32,1024]{2,1,0:T(8,128)(2,1)S(1)} %get-tuple-element.99), channel_id=1, source_target_pairs={{0,64},{1,65},{2,66},{3,67},{4,68},{5,69},{6,70},{7,71},{8,72},{9,... | collective-permute-start | bytes 786440 | tf_op jit(solution)/shard_map/ppermute | solution.py:40
  90.1 9.2 %collective-permute-start.20 = (bf16[4,32,1024]{2,1,0:T(8,128)(2,1)S(1)}, bf16[4,32,1024]{2,1,0:T(8,128)(2,1)S(1)}, u32[]{:S(2)}, u32[]{:S(2)}) collective-permute-start(bf16[4,32,1024]{2,1,0:T(8,128)(2,1)S(1)} %get-tuple-element.94), channel_id=1, source_target_pairs={{0,1},{1,2},{2,3},{3,0},{4,5},{5,6},{6,7},{7,4},{8,9},{9,10},{10,1... | collective-permute-start | bytes 786440 | tf_op jit(solution)/shard_map/ppermute | solution.py:40
  99.5 6.7 %collective-permute-start.26 = (f32[32,1024]{1,0:T(8,128)S(1)}, f32[32,1024]{1,0:T(8,128)S(1)}, u32[]{:S(2)}, u32[]{:S(2)}) collective-permute-start(f32[32,1024]{1,0:T(8,128)S(1)} %get-tuple-element.116), channel_id=1, source_target_pairs={{0,192},{1,193},{2,194},{3,195},{4,196},{5,197},{6,198},{7,199},{8... | collective-permute-start | bytes 393224 | tf_op jit(solution)/shard_map/ppermute | solution.py:40
  100.4 7.4 %collective-permute-start.27 = (f32[32,1024]{1,0:T(8,128)S(1)}, f32[32,1024]{1,0:T(8,128)S(1)}, u32[]{:S(2)}, u32[]{:S(2)}) collective-permute-start(f32[32,1024]{1,0:T(8,128)S(1)} %get-tuple-element.117), channel_id=1, source_target_pairs={{0,128},{1,129},{2,130},{3,131},{4,132},{5,133},{6,134},{7,135},{8... | collective-permute-start | bytes 393224 | tf_op jit(solution)/shard_map/ppermute | solution.py:40
  101.9 7.8 %collective-permute-start.28 = (f32[32,1024]{1,0:T(8,128)S(1)}, f32[32,1024]{1,0:T(8,128)S(1)}, u32[]{:S(2)}, u32[]{:S(2)}) collective-permute-start(f32[32,1024]{1,0:T(8,128)S(1)} %get-tuple-element.118), channel_id=1, source_target_pairs={{0,64},{1,65},{2,66},{3,67},{4,68},{5,69},{6,70},{7,71},{8,72},{9,... | collective-permute-start | bytes 393224 | tf_op jit(solution)/shard_map/ppermute | solution.py:40
  102.7 7.0 %collective-permute-start.29 = (f32[32,1024]{1,0:T(8,128)S(1)}, f32[32,1024]{1,0:T(8,128)S(1)}, u32[]{:S(2)}, u32[]{:S(2)}) collective-permute-start(f32[32,1024]{1,0:T(8,128)S(1)} %get-tuple-element.120), channel_id=1, source_target_pairs={{0,1},{1,2},{2,3},{3,0},{4,5},{5,6},{6,7},{7,4},{8,9},{9,10},{10,1... | collective-permute-start | bytes 393224 | tf_op jit(solution)/shard_map/ppermute | solution.py:40
  102.9 7.3 %collective-permute-start.30 = (f32[32,1024]{1,0:T(8,128)S(1)}, f32[32,1024]{1,0:T(8,128)S(1)}, u32[]{:S(2)}, u32[]{:S(2)}) collective-permute-start(f32[32,1024]{1,0:T(8,128)S(1)} %get-tuple-element.121), channel_id=1, source_target_pairs={{0,2},{1,3},{2,0},{3,1},{4,6},{5,7},{6,4},{7,5},{8,10},{9,11},{10,... | collective-permute-start | bytes 393224 | tf_op jit(solution)/shard_map/ppermute | solution.py:40
  106.2 5.4 %collective-permute-start.31 = (f32[32,1024]{1,0:T(8,128)S(1)}, f32[32,1024]{1,0:T(8,128)S(1)}, u32[]{:S(2)}, u32[]{:S(2)}) collective-permute-start(f32[32,1024]{1,0:T(8,128)S(1)} %get-tuple-element.122), channel_id=1, source_target_pairs={{0,3},{1,0},{2,1},{3,2},{4,7},{5,4},{6,5},{7,6},{8,11},{9,8},{10,9... | collective-permute-start | bytes 393224 | tf_op jit(solution)/shard_map/ppermute | solution.py:40
  112.3 8.8 %collective-permute-start.32 = (f32[3,64,128]{2,1,0:T(8,128)S(1)}, f32[3,64,128]{2,1,0:T(8,128)S(1)}, u32[]{:S(2)}, u32[]{:S(2)}) collective-permute-start(f32[3,64,128]{2,1,0:T(8,128)S(1)} %get-tuple-element.126), channel_id=1, source_target_pairs={{0,12},{1,13},{2,14},{3,15},{4,16},{5,17},{6,18},{7,19},{8,20},{9,... | collective-permute-start | bytes 294920 | tf_op jit(solution)/shard_map/ppermute | solution.py:40
  114.9 6.1 %collective-permute-start.33 = (f32[2,64,128]{2,1,0:T(8,128)S(1)}, f32[2,64,128]{2,1,0:T(8,128)S(1)}, u32[]{:S(2)}, u32[]{:S(2)}) collective-permute-start(f32[2,64,128]{2,1,0:T(8,128)S(1)} %get-tuple-element.127), channel_id=1, source_target_pairs={{0,20},{1,21},{2,22},{3,23},{4,24},{5,25},{6,26},{7,27},{8,28},{9,... | collective-permute-start | bytes 196616 | tf_op jit(solution)/shard_map/ppermute | solution.py:40
  121.0 6.0 %collective-permute-start.34 = (f32[1,64,128]{2,1,0:T(8,128)S(1)}, f32[1,64,128]{2,1,0:T(8,128)S(1)}, u32[]{:S(2)}, u32[]{:S(2)}) collective-permute-start(f32[1,64,128]{2,1,0:T(8,128)S(1)} %get-tuple-element.129), channel_id=1, source_target_pairs={{0,4},{1,5},{2,6},{3,7},{4,8},{5,9},{6,10},{7,11},{8,12},{9,13},{1... | collective-permute-start | bytes 98312 | tf_op jit(solution)/shard_map/ppermute | solution.py:40
  123.2 5.6 %collective-permute-start.35 = (f32[1,64,128]{2,1,0:T(8,128)S(1)}, f32[1,64,128]{2,1,0:T(8,128)S(1)}, u32[]{:S(2)}, u32[]{:S(2)}) collective-permute-start(f32[1,64,128]{2,1,0:T(8,128)S(1)} %get-tuple-element.130), channel_id=1, source_target_pairs={{0,28},{1,29},{2,30},{3,31},{4,0},{5,1},{6,2},{7,3},{8,4},{9,5},{1... | collective-permute-start | bytes 98312 | tf_op jit(solution)/shard_map/ppermute | solution.py:40
where the time goes:
time: 131 us; the launch traced here: 129 us
  starting transfers between devices  55.2 us (42%)
  Pallas kernels  34.8 us (27%)
  waiting for transfers between devices  33.1 us (25%)
  local copies, waits for them, and re-layouts  3.98 us (3%)
  other arithmetic  1.34 us (1%)
    ppermute x35, starting transfers between devices, send(): return lax.ppermute(value, AXES, pairs)  53.9 us
    ppermute x35, waiting for transfers between devices, send(): return lax.ppermute(value, AXES, pairs)  33.1 us
    pallas_call x1, Pallas kernels, target_of(): pl.pallas_call(target_kernel, out_shape=(jax.ShapeDtypeStruct((COLS, TOK)...  10.7 us
    pallas_call x1, Pallas kernels, terms_of(): pl.pallas_call(terms_kernel, grid_spec=pltpu.PrefetchScalarGridSpec(num_s...  7.25 us
    pallas_call x1, Pallas kernels, logits_of(): pl.pallas_call(logits_kernel, grid=(steps,), out_shape=(jax.ShapeDtypeStr...  7.16 us
    pallas_call x1, Pallas kernels, head_grad(): pl.pallas_call(head_kernel, grid=(D // width,), out_shape=jax.ShapeDtypeS...  4.69 us
  transfers between devices with their start and end apart: 36, of which 20 were waited for; matrix products, arithmetic and copies ran while one was open for 2% of the time, Pallas kernels for 20%

commit v1 on v0

--- a/solution.py
+++ b/solution.py
@@ -64,7 +64,7 @@
 
 
 def pack_kernel(place, owner, ids, scores, label, store_ids, store_logits, *outs):
-    y, c = place[2], place[3]
+    y, c = place[0], place[1]
     entries = jnp.concatenate([ids[...].astype(f32), scores[...].astype(f32)], axis=1).T
     teacher = jnp.concatenate([entries[:TOPK], entries[TOPK:]], axis=1)
     label_rows = jnp.concatenate([label[...].astype(f32), jnp.zeros((1, ROWS), f32)], axis=1)
@@ -123,6 +123,12 @@
     prob = jnp.exp(logp)
     tk_ref[...] = mixing * jnp.sum(prob * logp, axis=0, keepdims=True)
     prob_ref[...] = mixing * prob
+    ids_all = ids_ref[...]
+    summed = jnp.zeros((TOPK, TOK), f32)
+    for k in range(TOPK):
+        same = ids_all == ids_ref[pl.ds(k, 1), :]
+        summed = summed + jnp.where(same, prob_ref[pl.ds(k, 1), :], 0.0)
+    prob_ref[...] = summed
     step = 16
 
     def rows(i, carry):
@@ -130,15 +136,15 @@
         iota = lax.broadcasted_iota(jnp.int32, (step, TOK), 0) + first
         cols_own = iota + start_ref[0]
         cols_par = iota + start_ref[1]
-        own = jnp.where(cols_own == label, 1.0 - mixing, 0.0)
-        par = jnp.where(cols_par == label, 1.0 - mixing, 0.0)
+        own = jnp.zeros((step, TOK), f32)
+        par = jnp.zeros((step, TOK), f32)
         for k in range(TOPK):
             ids = ids_ref[pl.ds(k, 1), :]
             p = prob_ref[pl.ds(k, 1), :]
-            own = own + jnp.where(cols_own == ids, p, 0.0)
-            par = par + jnp.where(cols_par == ids, p, 0.0)
-        own_ref[pl.ds(first, step), :] = own
-        par_ref[pl.ds(first, step), :] = par
+            own = jnp.where(cols_own == ids, p, own)
+            par = jnp.where(cols_par == ids, p, par)
+        own_ref[pl.ds(first, step), :] = own + jnp.where(cols_own == label, 1.0 - mixing, 0.0)
+        par_ref[pl.ds(first, step), :] = par + jnp.where(cols_par == label, 1.0 - mixing, 0.0)
         return carry
 
     lax.fori_loop(0, COLS // step, rows, 0)
@@ -164,7 +170,7 @@
 
 
 def unpack_kernel(place, kept, digits, ids, logits, rows):
-    y, c = place[2], place[3]
+    c, y = place[0], place[1]
     high, middle, low, scores = (
         digits[:, k * TOPK : (k + 1) * TOPK].astype(f32) for k in range(4)
     )
@@ -204,7 +210,7 @@
 
 def logits_kernel(place, h0, h1, direct, swapped, h3, passed, wo, wp, to, tp, lo, lp, stats, hid):
     step = pl.program_id(0)
-    odd = place[1] & 1
+    odd = place[0]
     hid[0:ROWS, :] = h0[...]
     hid[ROWS : 2 * ROWS, :] = h1[...]
     hid[pl.ds(pl.multiple_of(2 * ROWS + odd * HALF, HALF), HALF), :] = direct[...]
@@ -368,7 +374,7 @@
 
 def terms_kernel(place, g_own, g_par, wo, wp, *rest):
     outs_a, outs_b = rest[0:4], rest[4:8]
-    x = place[1]
+    x = place[0]
 
     def features(ref, e):
         return jnp.concatenate(
@@ -497,12 +503,11 @@
 
 def body(hidden, head_weight, teacher_ids, teacher_logits, labels, store_ids, store_logits, owner):
     y, c, z, x = (lax.axis_index(name).astype(jnp.int32) for name in AXES)
-    place = jnp.stack([z, x, y, c])
     start = jnp.stack([index_of(y, c, z, x) * COLS, index_of(y, c + 1, z, x) * COLS])
     w_own = jnp.transpose(head_weight)
 
     packs = packs_of(
-        place, owner[:, 0], teacher_ids, teacher_logits, labels[None, :], store_ids, store_logits
+        jnp.stack([y, c]), owner[:, 0], teacher_ids, teacher_logits, labels[None, :], store_ids, store_logits
     )
     half = lax.dynamic_slice_in_dim(hidden, (x % 2) * HALF, HALF, 0)
     direct = send(half, dy=2)
@@ -512,7 +517,7 @@
     blocks = [hidden, send(nearby, dy=1), direct, swapped, send(nearby, dy=3)]
     w_par = send(w_own, dc=1)
     to, tp, tk, kept, passed = target_of(start, packs)
-    lo, lp, stats, hid = logits_of(place, blocks, passed, w_own, w_par, to, tp)
+    lo, lp, stats, hid = logits_of(jnp.stack([x % 2, x % 2]), blocks, passed, w_own, w_par, to, tp)
 
     parts = [stats] + [send(stats, dx=d) for d in range(1, NX)]
     stats = merged(parts, (0,) * NX)
@@ -522,12 +527,12 @@
     three, two = ring_merged(send(stats, dz=1), stats, send(stats, dz=-1))
     norm = final_norm(tk, [three, send(three, dz=-3), send(two, dz=3)])
     norm, hid_par = tied(norm, hid_par)
-    next_ids, next_logits = unpacked(place, kept, hid_par)
+    next_ids, next_logits = unpacked(jnp.stack([c, y]), kept, hid_par)
     token_loss = norm[1, :ROWS]
 
     go, gp, g_own, g_par = gradient_of(lo, lp, to, tp, norm)
     g_other = send(gp, dc=1)
-    terms = list(terms_of(place, g_own, g_par, w_own, w_par))
+    terms = list(terms_of(jnp.stack([x, z]), g_own, g_par, w_own, w_par))
     terms[1], g_other = tied(terms[1], g_other)
     a, b = terms[0:4], terms[4:8]
     a = [a[0]] + [send(a[d], dx=d) for d in range(1, NX)]
@@ -540,7 +545,7 @@
     grad_head = jnp.transpose(grad_head)
     a = [a[0]] + [send(a[d], dy=-d) for d in range(1, NY)]
     b = [b[0]] + [send(b[d], dx=d) for d in range(1, NX)]
-    own, ahead, behind, three, two = sum_second(place, a, b)
+    own, ahead, behind, three, two = sum_second(jnp.stack([z, x]), a, b)
     own, ahead, behind = sum_third(own, ahead, behind, send(three, dz=3), send(two, dz=-3))
     grad_hidden = own + send(ahead, dz=1) + send(behind, dz=-1)
     grad_hidden = grad_hidden.reshape(ROWS, 128).astype(bf16)

time: 131 us -> 130 us (level)
  Pallas kernels: 34.8 us -> 31.4 us
  waiting for transfers between devices: 33.1 us -> 35.6 us
    pallas_call x1, Pallas kernels: 10.7 us -> 7.25 us  [target_of(): pl.pallas_call(target_kernel, out_shape=(jax.ShapeDtypeStruct((COLS, TOK)...]
    ppermute x35, waiting for transfers between devices: 33.1 us -> 35.6 us  [send(): return lax.ppermute(value, AXES, pairs)]
  transfers between devices with their start and end apart: 36 -> 36, of which waited for: 20 -> 22; matrix products, arithmetic and copies ran while one was open for 2% -> 2% of each run, Pallas kernels for 20% -> 18%
where the time goes in v1:
time: 130 us; the launch traced here: 129 us
  starting transfers between devices  56 us (43%)
  waiting for transfers between devices  35.6 us (27%)
  Pallas kernels  31.4 us (24%)
  local copies, waits for them, and re-layouts  3.31 us (3%)
  other arithmetic  1.49 us (1%)
    ppermute x35, starting transfers between devices, send(): return lax.ppermute(value, AXES, pairs)  54.6 us
    ppermute x35, waiting for transfers between devices, send(): return lax.ppermute(value, AXES, pairs)  35.6 us
    pallas_call x1, Pallas kernels, target_of(): pl.pallas_call(target_kernel, out_shape=(jax.ShapeDtypeStruct((COLS, TOK)...  7.25 us
    pallas_call x1, Pallas kernels, terms_of(): pl.pallas_call(terms_kernel, grid_spec=pltpu.PrefetchScalarGridSpec(num_s...  7.25 us
    pallas_call x1, Pallas kernels, logits_of(): pl.pallas_call(logits_kernel, grid=(steps,), out_shape=(jax.ShapeDtypeStr...  7.22 us
    pallas_call x1, Pallas kernels, head_grad(): pl.pallas_call(head_kernel, grid=(D // width,), out_shape=jax.ShapeDtypeS...  4.7 us
  transfers between devices with their start and end apart: 36, of which 22 were waited for; matrix products, arithmetic and copies ran while one was open for 2% of the time, Pallas kernels for 18%

profile of v1, /device:TPU:2, one launch (start us, length us, event | category | flops | bytes accessed | tf_op | source)
XLA Modules:
  0.0 128.6 jit_solution(1968737196556734774)
XLA Ops:
  0.8 1.0 constant_dynamic-slice_fusion
  1.7 3.3 %collective-permute-start.3 = (bf16[32,4096]{1,0:T(8,128)(2,1)S(1)}, bf16[32,4096]{1,0:T(8,128)(2,1)S(1)}, u32[]{:S(2)}, u32[]{:S(2)}) collective-permute-start(bf16[32,4096]{1,0:T(8,128)(2,1)S(1)} %constant_dynamic-slice_fusion), channel_id=1, source_target_pairs={{0,128},{1,129},{2,130},{3,131},{4,132},{5,133},{6,134},{7,135},{8... | collective-permute-start | bytes 786440 | tf_op jit(solution)/shard_map/ppermute | solution.py:40
  5.0 0.6 pad_add_fusion.2
  5.6 2.3 %pack.1 = (f32[80,128]{1,0:T(8,128)}, f32[80,128]{1,0:T(8,128)}, f32[80,128]{1,0:T(8,128)}, f32[80,128]{1,0:T(8,128)}) custom-call(s32[2]{0:T(128)} %get-tuple-element.133.place, s32[16]{0:T(128)} %bitcast.19, s32[64,64]{1,0:T(8,128)} %ids.1, bf16[64,64]{1,0:T(8,128)(2,1)} %scores.1, s32[1,64]{1,0:T(1,128)} %bitcast.20, s32[16,64]{1,0:T(8,128)} %store_ids.1, ...), custom_call_target="tpu_custom_call" | custom-call | tf_op jit(solution)/shard_map/pack/pallas_call | solution.py:98
  7.8 0.7 collective-permute-start
  8.5 1.8 %collective-permute-start.1 = (f32[80,128]{1,0:T(8,128)}, f32[80,128]{1,0:T(8,128)S(1)}, u32[]{:S(2)}, u32[]{:S(2)}) collective-permute-start(f32[80,128]{1,0:T(8,128)} %get-tuple-element.71), channel_id=1, source_target_pairs={{0,128},{1,129},{2,130},{3,131},{4,132},{5,133},{6,134},{7,135},{8... | collective-permute-start | bytes 122888 | tf_op jit(solution)/shard_map/ppermute | solution.py:40
  10.4 0.9 collective-permute-start.2
  11.3 2.4 %collective-permute-done.p1 = f32[80,128]{1,0:T(8,128)S(1)} collective-permute-done((f32[80,128]{1,0:T(8,128)}, f32[80,128]{1,0:T(8,128)S(1)}, u32[]{:S(2)}, u32[]{:S(2)}) %collective-permute-start) | collective-permute-done | bytes 40992 | tf_op jit(solution)/shard_map/ppermute | solution.py:40
  13.7 0.5 collective-permute-done.1.p2
  14.2 0.3 collective-permute-done.2.p3
  14.6 2.6 %collective-permute-start.6 = (bf16[64,4096]{1,0:T(8,128)(2,1)}, bf16[64,4096]{1,0:T(8,128)(2,1)S(1)}, u32[]{:S(2)}, u32[]{:S(2)}) collective-permute-start(bf16[64,4096]{1,0:T(8,128)(2,1)} %h0.1), channel_id=1, source_target_pairs={{0,192},{1,193},{2,194},{3,195},{4,196},{5,197},{6,198},{7,199},{8... | collective-permute-start | bytes 1572872 | tf_op jit(solution)/shard_map/ppermute | solution.py:40
  17.1 1.4 %collective-permute-start.5 = (bf16[32,4096]{1,0:T(8,128)(2,1)S(1)}, bf16[32,4096]{1,0:T(8,128)(2,1)S(1)}, u32[]{:S(2)}, u32[]{:S(2)}) collective-permute-start(bf16[32,4096]{1,0:T(8,128)(2,1)S(1)} %collective-permute-done.3.direct), channel_id=1, source_target_pairs={{0,1},{1,0},{2,3},{3,2},{4,5},{5,4},{6,7},{7,6},{8,9},{9,8},{10,11... | collective-permute-start | bytes 786440 | tf_op jit(solution)/shard_map/ppermute | solution.py:51
  18.7 0.8 copy-done.2
  19.4 7.3 %target.1 = (f32[592,256]{1,0:T(8,128)S(1)}, f32[592,256]{1,0:T(8,128)S(1)}, f32[1,256]{1,0:T(1,128)S(1)}, f32[16,128]{1,0:T(8,128)S(1)}, bf16[16,256]{1,0:T(8,128)(2,1)S(1)}) custom-call(s32[2]{0:T(128)S(1)} %pad_add_fusion.3.start_ref, f32[80,128]{1,0:T(8,128)S(1)} %copy-done.2, f32[80,128]{1,0:T(8,128)S(1)} %collective-permute-done.p1, ...), custom_call_target="tpu_custom_call" | custom-call | flops 1000000 | bytes 1400000 | tf_op jit(solution)/shard_map/target/pallas_call | solution.py:154
  26.7 0.9 collective-permute-done.6.h3
  27.7 3.2 %collective-permute-done.4.h1 = bf16[64,4096]{1,0:T(8,128)(2,1)S(1)} collective-permute-done((bf16[64,4096]{1,0:T(8,128)(2,1)}, bf16[64,4096]{1,0:T(8,128)(2,1)S(1)}, u32[]{:S(2)}, u32[]{:S(2)}) %collective-permute-start.4) | collective-permute-done | bytes 524320 | tf_op jit(solution)/shard_map/ppermute | solution.py:40
  30.9 1.0 copy-done.1
  31.9 7.2 %logits.1 = (f32[592,256]{1,0:T(8,128)S(1)}, f32[592,256]{1,0:T(8,128)S(1)}, f32[8,256]{1,0:T(8,128)S(1)}, bf16[272,4096]{1,0:T(8,128)(2,1)}) custom-call(s32[2]{0:T(128)S(1)} %pad_add_fusion.1.place, bf16[64,4096]{1,0:T(8,128)(2,1)S(1)} %copy-done.1, bf16[64,4096]{1,0:T(8,128)(2,1)S(1)} %collective-permute-done.4.h1, ...), custom_call_target="tpu_custom_call" | custom-call | flops 2483027968 | bytes 14000000 | tf_op jit(solution)/shard_map/logits/pallas_call | solution.py:255
  39.1 1.6 %collective-permute-start.10 = (f32[8,256]{1,0:T(8,128)S(1)}, f32[8,256]{1,0:T(8,128)S(1)}, u32[]{:S(2)}, u32[]{:S(2)}) collective-permute-start(f32[8,256]{1,0:T(8,128)S(1)} %get-tuple-element.85.refs_0_), channel_id=1, source_target_pairs={{0,3},{1,0},{2,1},{3,2},{4,7},{5,4},{6,5},{7,6},{8,11},{9,8},{10,9... | collective-permute-start | bytes 24584 | tf_op jit(solution)/shard_map/ppermute | solution.py:40
  40.7 1.4 %collective-permute-start.9 = (f32[8,256]{1,0:T(8,128)S(1)}, f32[8,256]{1,0:T(8,128)S(1)}, u32[]{:S(2)}, u32[]{:S(2)}) collective-permute-start(f32[8,256]{1,0:T(8,128)S(1)} %get-tuple-element.85.refs_0_), channel_id=1, source_target_pairs={{0,2},{1,3},{2,0},{3,1},{4,6},{5,7},{6,4},{7,5},{8,10},{9,11},{10,... | collective-permute-start | bytes 24584 | tf_op jit(solution)/shard_map/ppermute | solution.py:40
  42.1 1.8 %collective-permute-start.8 = (f32[8,256]{1,0:T(8,128)S(1)}, f32[8,256]{1,0:T(8,128)S(1)}, u32[]{:S(2)}, u32[]{:S(2)}) collective-permute-start(f32[8,256]{1,0:T(8,128)S(1)} %get-tuple-element.85.refs_0_), channel_id=1, source_target_pairs={{0,1},{1,2},{2,3},{3,0},{4,5},{5,6},{6,7},{7,4},{8,9},{9,10},{10,1... | collective-permute-start | bytes 24584 | tf_op jit(solution)/shard_map/ppermute | solution.py:40
  43.9 2.0 %collective-permute-done.9.refs_2_ = f32[8,256]{1,0:T(8,128)S(1)} collective-permute-done((f32[8,256]{1,0:T(8,128)S(1)}, f32[8,256]{1,0:T(8,128)S(1)}, u32[]{:S(2)}, u32[]{:S(2)}) %collective-permute-start.9) | collective-permute-done | bytes 8224 | tf_op jit(solution)/shard_map/ppermute | solution.py:40
  46.0 1.7 %collective-permute-start.12 = (f32[8,256]{1,0:T(8,128)S(1)}, f32[8,256]{1,0:T(8,128)S(1)}, u32[]{:S(2)}, u32[]{:S(2)}) collective-permute-start(f32[8,256]{1,0:T(8,128)S(1)} %merge.2.refs_0_), channel_id=1, source_target_pairs={{0,128},{1,129},{2,130},{3,131},{4,132},{5,133},{6,134},{7,135},{8... | collective-permute-start | bytes 24584 | tf_op jit(solution)/shard_map/ppermute | solution.py:40
  47.7 1.5 %collective-permute-start.11 = (f32[8,256]{1,0:T(8,128)S(1)}, f32[8,256]{1,0:T(8,128)S(1)}, u32[]{:S(2)}, u32[]{:S(2)}) collective-permute-start(f32[8,256]{1,0:T(8,128)S(1)} %merge.2.refs_0_), channel_id=1, source_target_pairs={{0,192},{1,193},{2,194},{3,195},{4,196},{5,197},{6,198},{7,199},{8... | collective-permute-start | bytes 24584 | tf_op jit(solution)/shard_map/ppermute | solution.py:40
  49.2 1.6 %collective-permute-done.13.refs_3_ = f32[8,256]{1,0:T(8,128)S(1)} collective-permute-done((f32[8,256]{1,0:T(8,128)S(1)}, f32[8,256]{1,0:T(8,128)S(1)}, u32[]{:S(2)}, u32[]{:S(2)}) %collective-permute-start.13) | collective-permute-done | bytes 8224 | tf_op jit(solution)/shard_map/ppermute | solution.py:40
  50.8 0.6 collective-permute-done.12.refs_2_
  51.4 0.4 collective-permute-done.11.refs_1_
  51.9 5.8 %collective-permute-start.15 = (f32[8,256]{1,0:T(8,128)S(1)}, f32[8,256]{1,0:T(8,128)S(1)}, u32[]{:S(2)}, u32[]{:S(2)}) collective-permute-start(f32[8,256]{1,0:T(8,128)S(1)} %merge.3.here), channel_id=1, source_target_pairs={{0,28},{1,29},{2,30},{3,31},{4,0},{5,1},{6,2},{7,3},{8,4},{9,5},{1... | collective-permute-start | bytes 24584 | tf_op jit(solution)/shard_map/ppermute | solution.py:40
  57.7 1.4 %collective-permute-done.15.after = f32[8,256]{1,0:T(8,128)S(1)} collective-permute-done((f32[8,256]{1,0:T(8,128)S(1)}, f32[8,256]{1,0:T(8,128)S(1)}, u32[]{:S(2)}, u32[]{:S(2)}) %collective-permute-start.15) | collective-permute-done | bytes 8224 | tf_op jit(solution)/shard_map/ppermute | solution.py:40
  59.0 3.5 %collective-permute-done.14.before = f32[8,256]{1,0:T(8,128)S(1)} collective-permute-done((f32[8,256]{1,0:T(8,128)S(1)}, f32[8,256]{1,0:T(8,128)S(1)}, u32[]{:S(2)}, u32[]{:S(2)}) %collective-permute-start.14) | collective-permute-done | bytes 8224 | tf_op jit(solution)/shard_map/ppermute | solution.py:40
  62.7 5.0 %collective-permute-start.16 = (f32[8,256]{1,0:T(8,128)S(1)}, f32[8,256]{1,0:T(8,128)S(1)}, u32[]{:S(2)}, u32[]{:S(2)}) collective-permute-start(f32[8,256]{1,0:T(8,128)S(1)} %get-tuple-element.86.refs_0_), channel_id=1, source_target_pairs={{0,20},{1,21},{2,22},{3,23},{4,24},{5,25},{6,26},{7,27},{8,28},{9,... | collective-permute-start | bytes 24584 | tf_op jit(solution)/shard_map/ppermute | solution.py:40
  67.8 1.5 %collective-permute-done.17.refs_2_ = f32[8,256]{1,0:T(8,128)S(1)} collective-permute-done((f32[8,256]{1,0:T(8,128)S(1)}, f32[8,256]{1,0:T(8,128)S(1)}, u32[]{:S(2)}, u32[]{:S(2)}) %collective-permute-start.17) | collective-permute-done | bytes 8224 | tf_op jit(solution)/shard_map/ppermute | solution.py:40
  69.3 0.3 gradient.1
  69.8 7.3 %terms.1 = (f32[4,32,1024]{2,1,0:T(8,128)S(1)}, bf16[4,32,1024]{2,1,0:T(8,128)(2,1)S(1)}, bf16[4,32,1024]{2,1,0:T(8,128)(2,1)S(1)}, bf16[4,32,1024]{2,1,0:T(8,12...) custom-call(s32[2]{0:T(128)S(1)} %pad_add_fusion.place, ...), custom_call_target="tpu_custom_call" | custom-call | flops 2483027968 | bytes 16000000 | tf_op jit(solution)/shard_map/terms/pallas_call | solution.py:403
  77.1 1.6 %collective-permute-start.21 = (bf16[4,32,1024]{2,1,0:T(8,128)(2,1)S(1)}, bf16[4,32,1024]{2,1,0:T(8,128)(2,1)S(1)}, u32[]{:S(2)}, u32[]{:S(2)}) collective-permute-start(bf16[4,32,1024]{2,1,0:T(8,128)(2,1)S(1)} %get-tuple-element.95), channel_id=1, source_target_pairs={{0,2},{1,3},{2,0},{3,1},{4,6},{5,7},{6,4},{7,5},{8,10},{9,11},{10,... | collective-permute-start | bytes 786440 | tf_op jit(solution)/shard_map/ppermute | solution.py:40
  78.6 2.4 %collective-permute-start.22 = (bf16[4,32,1024]{2,1,0:T(8,128)(2,1)S(1)}, bf16[4,32,1024]{2,1,0:T(8,128)(2,1)S(1)}, u32[]{:S(2)}, u32[]{:S(2)}) collective-permute-start(bf16[4,32,1024]{2,1,0:T(8,128)(2,1)S(1)} %get-tuple-element.96), channel_id=1, source_target_pairs={{0,3},{1,0},{2,1},{3,2},{4,7},{5,4},{6,5},{7,6},{8,11},{9,8},{10,9... | collective-permute-start | bytes 786440 | tf_op jit(solution)/shard_map/ppermute | solution.py:40
  81.0 2.6 %collective-permute-start.23 = (bf16[4,32,1024]{2,1,0:T(8,128)(2,1)S(1)}, bf16[4,32,1024]{2,1,0:T(8,128)(2,1)S(1)}, u32[]{:S(2)}, u32[]{:S(2)}) collective-permute-start(bf16[4,32,1024]{2,1,0:T(8,128)(2,1)S(1)} %get-tuple-element.97), channel_id=1, source_target_pairs={{0,192},{1,193},{2,194},{3,195},{4,196},{5,197},{6,198},{7,199},{8... | collective-permute-start | bytes 786440 | tf_op jit(solution)/shard_map/ppermute | solution.py:40
  83.6 1.4 %collective-permute-start.24 = (bf16[4,32,1024]{2,1,0:T(8,128)(2,1)S(1)}, bf16[4,32,1024]{2,1,0:T(8,128)(2,1)S(1)}, u32[]{:S(2)}, u32[]{:S(2)}) collective-permute-start(bf16[4,32,1024]{2,1,0:T(8,128)(2,1)S(1)} %get-tuple-element.98), channel_id=1, source_target_pairs={{0,128},{1,129},{2,130},{3,131},{4,132},{5,133},{6,134},{7,135},{8... | collective-permute-start | bytes 786440 | tf_op jit(solution)/shard_map/ppermute | solution.py:40
  85.0 2.8 %collective-permute-done.21.refs_2_ = bf16[4,32,1024]{2,1,0:T(8,128)(2,1)S(1)} collective-permute-done((bf16[4,32,1024]{2,1,0:T(8,128)(2,1)S(1)}, bf16[4,32,1024]{2,1,0:T(8,128)(2,1)S(1)}, u32[]{:S(2)}, u32[]{:S(2)}) %collective-permute-start.21) | collective-permute-done | bytes 262176 | tf_op jit(solution)/shard_map/ppermute | solution.py:40
  87.8 1.4 %collective-permute-start.20 = (bf16[4,32,1024]{2,1,0:T(8,128)(2,1)S(1)}, bf16[4,32,1024]{2,1,0:T(8,128)(2,1)S(1)}, u32[]{:S(2)}, u32[]{:S(2)}) collective-permute-start(bf16[4,32,1024]{2,1,0:T(8,128)(2,1)S(1)} %get-tuple-element.94), channel_id=1, source_target_pairs={{0,1},{1,2},{2,3},{3,0},{4,5},{5,6},{6,7},{7,4},{8,9},{9,10},{10,1... | collective-permute-start | bytes 786440 | tf_op jit(solution)/shard_map/ppermute | solution.py:40
  89.2 1.4 %unpack.1 = (s32[32,64]{1,0:T(8,128)}, bf16[32,64]{1,0:T(8,128)(2,1)}) custom-call(s32[2]{0:T(128)S(1)} %get-tuple-element.134.place, f32[16,128]{1,0:T(8,128)S(1)} %get-tuple-element.103.kept, bf16[272,4096]{1,0:T(8,128)(2,1)S(1)} %collective-permute-done.18.h1.digits), custom_call_target="tpu_custom_call" | custom-call | tf_op jit(solution)/shard_map/unpack/pallas_call | solution.py:189
  90.5 4.7 %head_grad.1 = bf16[592,4096]{1,0:T(8,128)(2,1)} custom-call(bf16[592,256]{1,0:T(8,128)(2,1)S(1)} %get-tuple-element.100.g0, bf16[592,256]{1,0:T(8,128)(2,1)S(1)} %collective-permute-done.19.g1, bf16[272,4096]{1,0:T(8,128)(2,1)S(1)} %copy-done, bf16[272,4096]{1,0:T(8,128)(2,1)S(1)} %collective-permute-done.18.h1.digits), custom_call_target="tpu_custom_call" | custom-call | flops 2483027968 | bytes 10000000 | tf_op jit(solution)/shard_map/head_grad/pallas_call | solution.py:487
  95.2 3.4 %collective-permute-done.25.refs_7_ = bf16[4,32,1024]{2,1,0:T(8,128)(2,1)S(1)} collective-permute-done((bf16[4,32,1024]{2,1,0:T(8,128)(2,1)S(1)}, bf16[4,32,1024]{2,1,0:T(8,128)(2,1)S(1)}, u32[]{:S(2)}, u32[]{:S(2)}) %collective-permute-start.25) | collective-permute-done | bytes 262176 | tf_op jit(solution)/shard_map/ppermute | solution.py:40
  98.6 0.2 sum_first.1
  98.8 0.9 collective-permute-start.26
  99.7 1.4 %collective-permute-start.27 = (f32[32,1024]{1,0:T(8,128)S(1)}, f32[32,1024]{1,0:T(8,128)S(1)}, u32[]{:S(2)}, u32[]{:S(2)}) collective-permute-start(f32[32,1024]{1,0:T(8,128)S(1)} %get-tuple-element.117), channel_id=1, source_target_pairs={{0,128},{1,129},{2,130},{3,131},{4,132},{5,133},{6,134},{7,135},{8... | collective-permute-start | bytes 393224 | tf_op jit(solution)/shard_map/ppermute | solution.py:40
  101.1 0.8 collective-permute-start.28
  102.0 0.2 collective-permute-start.29
  102.2 3.3 %collective-permute-start.30 = (f32[32,1024]{1,0:T(8,128)S(1)}, f32[32,1024]{1,0:T(8,128)S(1)}, u32[]{:S(2)}, u32[]{:S(2)}) collective-permute-start(f32[32,1024]{1,0:T(8,128)S(1)} %get-tuple-element.121), channel_id=1, source_target_pairs={{0,2},{1,3},{2,0},{3,1},{4,6},{5,7},{6,4},{7,5},{8,10},{9,11},{10,... | collective-permute-start | bytes 393224 | tf_op jit(solution)/shard_map/ppermute | solution.py:40
  105.5 0.8 collective-permute-start.31
  106.4 0.8 collective-permute-done.27.refs_2_
  107.2 1.8 %collective-permute-done.28.refs_3_ = f32[32,1024]{1,0:T(8,128)S(1)} collective-permute-done((f32[32,1024]{1,0:T(8,128)S(1)}, f32[32,1024]{1,0:T(8,128)S(1)}, u32[]{:S(2)}, u32[]{:S(2)}) %collective-permute-start.28) | collective-permute-done | bytes 131104 | tf_op jit(solution)/shard_map/ppermute | solution.py:40
  109.0 0.5 collective-permute-done.30.refs_6_
  109.5 1.4 %collective-permute-done.31.refs_7_ = f32[32,1024]{1,0:T(8,128)S(1)} collective-permute-done((f32[32,1024]{1,0:T(8,128)S(1)}, f32[32,1024]{1,0:T(8,128)S(1)}, u32[]{:S(2)}, u32[]{:S(2)}) %collective-permute-start.31) | collective-permute-done | bytes 131104 | tf_op jit(solution)/shard_map/ppermute | solution.py:40
  110.9 0.7 sum_second.1
  111.5 2.7 %collective-permute-start.32 = (f32[3,64,128]{2,1,0:T(8,128)S(1)}, f32[3,64,128]{2,1,0:T(8,128)S(1)}, u32[]{:S(2)}, u32[]{:S(2)}) collective-permute-start(f32[3,64,128]{2,1,0:T(8,128)S(1)} %get-tuple-element.126), channel_id=1, source_target_pairs={{0,12},{1,13},{2,14},{3,15},{4,16},{5,17},{6,18},{7,19},{8,20},{9,... | collective-permute-start | bytes 294920 | tf_op jit(solution)/shard_map/ppermute | solution.py:40
  114.2 2.5 %collective-permute-start.33 = (f32[2,64,128]{2,1,0:T(8,128)S(1)}, f32[2,64,128]{2,1,0:T(8,128)S(1)}, u32[]{:S(2)}, u32[]{:S(2)}) collective-permute-start(f32[2,64,128]{2,1,0:T(8,128)S(1)} %get-tuple-element.127), channel_id=1, source_target_pairs={{0,20},{1,21},{2,22},{3,23},{4,24},{5,25},{6,26},{7,27},{8,28},{9,... | collective-permute-start | bytes 196616 | tf_op jit(solution)/shard_map/ppermute | solution.py:40
  116.7 3.6 %collective-permute-done.33.two = f32[2,64,128]{2,1,0:T(8,128)S(1)} collective-permute-done((f32[2,64,128]{2,1,0:T(8,128)S(1)}, f32[2,64,128]{2,1,0:T(8,128)S(1)}, u32[]{:S(2)}, u32[]{:S(2)}) %collective-permute-start.33) | collective-permute-done | bytes 65568 | tf_op jit(solution)/shard_map/ppermute | solution.py:40
  120.3 2.1 %collective-permute-start.34 = (f32[1,64,128]{2,1,0:T(8,128)S(1)}, f32[1,64,128]{2,1,0:T(8,128)S(1)}, u32[]{:S(2)}, u32[]{:S(2)}) collective-permute-start(f32[1,64,128]{2,1,0:T(8,128)S(1)} %get-tuple-element.129), channel_id=1, source_target_pairs={{0,4},{1,5},{2,6},{3,7},{4,8},{5,9},{6,10},{7,11},{8,12},{9,13},{1... | collective-permute-start | bytes 98312 | tf_op jit(solution)/shard_map/ppermute | solution.py:40
  122.4 2.1 %collective-permute-start.35 = (f32[1,64,128]{2,1,0:T(8,128)S(1)}, f32[1,64,128]{2,1,0:T(8,128)S(1)}, u32[]{:S(2)}, u32[]{:S(2)}) collective-permute-start(f32[1,64,128]{2,1,0:T(8,128)S(1)} %get-tuple-element.130), channel_id=1, source_target_pairs={{0,28},{1,29},{2,30},{3,31},{4,0},{5,1},{6,2},{7,3},{8,4},{9,5},{1... | collective-permute-start | bytes 98312 | tf_op jit(solution)/shard_map/ppermute | solution.py:40
  124.6 0.5 slice_bitcast_fusion
  125.1 1.3 %collective-permute-done.34 = f32[1,64,128]{2,1,0:T(8,128)S(1)} collective-permute-done((f32[1,64,128]{2,1,0:T(8,128)S(1)}, f32[1,64,128]{2,1,0:T(8,128)S(1)}, u32[]{:S(2)}, u32[]{:S(2)}) %collective-permute-start.34) | collective-permute-done | bytes 32800 | tf_op jit(solution)/shard_map/ppermute | solution.py:40
  126.4 1.6 %collective-permute-done.35 = f32[1,64,128]{2,1,0:T(8,128)S(1)} collective-permute-done((f32[1,64,128]{2,1,0:T(8,128)S(1)}, f32[1,64,128]{2,1,0:T(8,128)S(1)}, u32[]{:S(2)}, u32[]{:S(2)}) %collective-permute-start.35) | collective-permute-done | bytes 32800 | tf_op jit(solution)/shard_map/ppermute | solution.py:40
  128.0 0.6 fusion
  (36 shorter events, 0.9 us)
Async XLA Ops:
  0.6 30.2 %collective-permute-start.7 = (bf16[592,4096]{1,0:T(8,128)(2,1)}, bf16[592,4096]{1,0:T(8,128)(2,1)}, u32[]{:S(2)}, u32[]{:S(2)}) collective-permute-start(bf16[592,4096]{1,0:T(8,128)(2,1)} %bitcast.15), channel_id=1, source_target_pairs={{0,32},{1,33},{2,34},{3,35},{4,36},{5,37},{6,38},{7,39},{8,40},{9,... | collective-permute-start | bytes 14549000 | tf_op jit(solution)/shard_map/ppermute | solution.py:40
  1.7 12.8 %collective-permute-start.3 = (bf16[32,4096]{1,0:T(8,128)(2,1)S(1)}, bf16[32,4096]{1,0:T(8,128)(2,1)S(1)}, u32[]{:S(2)}, u32[]{:S(2)}) collective-permute-start(bf16[32,4096]{1,0:T(8,128)(2,1)S(1)} %constant_dynamic-slice_fusion), channel_id=1, source_target_pairs={{0,128},{1,129},{2,130},{3,131},{4,132},{5,133},{6,134},{7,135},{8... | collective-permute-start | bytes 786440 | tf_op jit(solution)/shard_map/ppermute | solution.py:40
  7.8 5.9 %collective-permute-start = (f32[80,128]{1,0:T(8,128)}, f32[80,128]{1,0:T(8,128)S(1)}, u32[]{:S(2)}, u32[]{:S(2)}) collective-permute-start(f32[80,128]{1,0:T(8,128)} %get-tuple-element.70), channel_id=1, source_target_pairs={{0,64},{1,65},{2,66},{3,67},{4,68},{5,69},{6,70},{7,71},{8,72},{9,... | collective-permute-start | bytes 122888 | tf_op jit(solution)/shard_map/ppermute | solution.py:40
  8.5 5.7 %collective-permute-start.1 = (f32[80,128]{1,0:T(8,128)}, f32[80,128]{1,0:T(8,128)S(1)}, u32[]{:S(2)}, u32[]{:S(2)}) collective-permute-start(f32[80,128]{1,0:T(8,128)} %get-tuple-element.71), channel_id=1, source_target_pairs={{0,128},{1,129},{2,130},{3,131},{4,132},{5,133},{6,134},{7,135},{8... | collective-permute-start | bytes 122888 | tf_op jit(solution)/shard_map/ppermute | solution.py:40
  10.4 4.2 %collective-permute-start.2 = (f32[80,128]{1,0:T(8,128)}, f32[80,128]{1,0:T(8,128)S(1)}, u32[]{:S(2)}, u32[]{:S(2)}) collective-permute-start(f32[80,128]{1,0:T(8,128)} %get-tuple-element.72), channel_id=1, source_target_pairs={{0,192},{1,193},{2,194},{3,195},{4,196},{5,197},{6,198},{7,199},{8... | collective-permute-start | bytes 122888 | tf_op jit(solution)/shard_map/ppermute | solution.py:40
  14.6 13.1 %collective-permute-start.6 = (bf16[64,4096]{1,0:T(8,128)(2,1)}, bf16[64,4096]{1,0:T(8,128)(2,1)S(1)}, u32[]{:S(2)}, u32[]{:S(2)}) collective-permute-start(bf16[64,4096]{1,0:T(8,128)(2,1)} %h0.1), channel_id=1, source_target_pairs={{0,192},{1,193},{2,194},{3,195},{4,196},{5,197},{6,198},{7,199},{8... | collective-permute-start | bytes 1572872 | tf_op jit(solution)/shard_map/ppermute | solution.py:40
  17.1 13.7 %collective-permute-start.4 = (bf16[64,4096]{1,0:T(8,128)(2,1)}, bf16[64,4096]{1,0:T(8,128)(2,1)S(1)}, u32[]{:S(2)}, u32[]{:S(2)}) collective-permute-start(bf16[64,4096]{1,0:T(8,128)(2,1)} %h0.1), channel_id=1, source_target_pairs={{0,64},{1,65},{2,66},{3,67},{4,68},{5,69},{6,70},{7,71},{8,72},{9,... | collective-permute-start | bytes 1572872 | tf_op jit(solution)/shard_map/ppermute | solution.py:40
  17.1 9.6 %collective-permute-start.5 = (bf16[32,4096]{1,0:T(8,128)(2,1)S(1)}, bf16[32,4096]{1,0:T(8,128)(2,1)S(1)}, u32[]{:S(2)}, u32[]{:S(2)}) collective-permute-start(bf16[32,4096]{1,0:T(8,128)(2,1)S(1)} %collective-permute-done.3.direct), channel_id=1, source_target_pairs={{0,1},{1,0},{2,3},{3,2},{4,5},{5,4},{6,7},{7,6},{8,9},{9,8},{10,11... | collective-permute-start | bytes 786440 | tf_op jit(solution)/shard_map/ppermute | solution.py:51
  18.7 0.8 copy-start.2
  30.9 1.0 copy-start.1
  39.1 30.2 %collective-permute-start.18 = (bf16[272,4096]{1,0:T(8,128)(2,1)}, bf16[272,4096]{1,0:T(8,128)(2,1)S(1)}, u32[]{:S(2)}, u32[]{:S(2)}) collective-permute-start(bf16[272,4096]{1,0:T(8,128)(2,1)} %get-tuple-element.88.h0), channel_id=1, source_target_pairs={{0,32},{1,33},{2,34},{3,35},{4,36},{5,37},{6,38},{7,39},{8,40},{9,... | collective-permute-start | bytes 6684680 | tf_op jit(solution)/shard_map/ppermute | solution.py:40
  39.1 4.8 %collective-permute-start.10 = (f32[8,256]{1,0:T(8,128)S(1)}, f32[8,256]{1,0:T(8,128)S(1)}, u32[]{:S(2)}, u32[]{:S(2)}) collective-permute-start(f32[8,256]{1,0:T(8,128)S(1)} %get-tuple-element.85.refs_0_), channel_id=1, source_target_pairs={{0,3},{1,0},{2,1},{3,2},{4,7},{5,4},{6,5},{7,6},{8,11},{9,8},{10,9... | collective-permute-start | bytes 24584 | tf_op jit(solution)/shard_map/ppermute | solution.py:40
  40.7 5.2 %collective-permute-start.9 = (f32[8,256]{1,0:T(8,128)S(1)}, f32[8,256]{1,0:T(8,128)S(1)}, u32[]{:S(2)}, u32[]{:S(2)}) collective-permute-start(f32[8,256]{1,0:T(8,128)S(1)} %get-tuple-element.85.refs_0_), channel_id=1, source_target_pairs={{0,2},{1,3},{2,0},{3,1},{4,6},{5,7},{6,4},{7,5},{8,10},{9,11},{10,... | collective-permute-start | bytes 24584 | tf_op jit(solution)/shard_map/ppermute | solution.py:40
  42.1 3.8 %collective-permute-start.8 = (f32[8,256]{1,0:T(8,128)S(1)}, f32[8,256]{1,0:T(8,128)S(1)}, u32[]{:S(2)}, u32[]{:S(2)}) collective-permute-start(f32[8,256]{1,0:T(8,128)S(1)} %get-tuple-element.85.refs_0_), channel_id=1, source_target_pairs={{0,1},{1,2},{2,3},{3,0},{4,5},{5,6},{6,7},{7,4},{8,9},{9,10},{10,1... | collective-permute-start | bytes 24584 | tf_op jit(solution)/shard_map/ppermute | solution.py:40
  45.9 4.9 %collective-permute-start.13 = (f32[8,256]{1,0:T(8,128)S(1)}, f32[8,256]{1,0:T(8,128)S(1)}, u32[]{:S(2)}, u32[]{:S(2)}) collective-permute-start(f32[8,256]{1,0:T(8,128)S(1)} %merge.2.refs_0_), channel_id=1, source_target_pairs={{0,64},{1,65},{2,66},{3,67},{4,68},{5,69},{6,70},{7,71},{8,72},{9,... | collective-permute-start | bytes 24584 | tf_op jit(solution)/shard_map/ppermute | solution.py:40
  46.0 5.4 %collective-permute-start.12 = (f32[8,256]{1,0:T(8,128)S(1)}, f32[8,256]{1,0:T(8,128)S(1)}, u32[]{:S(2)}, u32[]{:S(2)}) collective-permute-start(f32[8,256]{1,0:T(8,128)S(1)} %merge.2.refs_0_), channel_id=1, source_target_pairs={{0,128},{1,129},{2,130},{3,131},{4,132},{5,133},{6,134},{7,135},{8... | collective-permute-start | bytes 24584 | tf_op jit(solution)/shard_map/ppermute | solution.py:40
  47.7 4.1 %collective-permute-start.11 = (f32[8,256]{1,0:T(8,128)S(1)}, f32[8,256]{1,0:T(8,128)S(1)}, u32[]{:S(2)}, u32[]{:S(2)}) collective-permute-start(f32[8,256]{1,0:T(8,128)S(1)} %merge.2.refs_0_), channel_id=1, source_target_pairs={{0,192},{1,193},{2,194},{3,195},{4,196},{5,197},{6,198},{7,199},{8... | collective-permute-start | bytes 24584 | tf_op jit(solution)/shard_map/ppermute | solution.py:40
  51.9 7.2 %collective-permute-start.15 = (f32[8,256]{1,0:T(8,128)S(1)}, f32[8,256]{1,0:T(8,128)S(1)}, u32[]{:S(2)}, u32[]{:S(2)}) collective-permute-start(f32[8,256]{1,0:T(8,128)S(1)} %merge.3.here), channel_id=1, source_target_pairs={{0,28},{1,29},{2,30},{3,31},{4,0},{5,1},{6,2},{7,3},{8,4},{9,5},{1... | collective-permute-start | bytes 24584 | tf_op jit(solution)/shard_map/ppermute | solution.py:40
  57.7 4.9 %collective-permute-start.14 = (f32[8,256]{1,0:T(8,128)S(1)}, f32[8,256]{1,0:T(8,128)S(1)}, u32[]{:S(2)}, u32[]{:S(2)}) collective-permute-start(f32[8,256]{1,0:T(8,128)S(1)} %merge.3.here), channel_id=1, source_target_pairs={{0,4},{1,5},{2,6},{3,7},{4,8},{5,9},{6,10},{7,11},{8,12},{9,13},{1... | collective-permute-start | bytes 24584 | tf_op jit(solution)/shard_map/ppermute | solution.py:40
  62.6 6.7 %collective-permute-start.17 = (f32[8,256]{1,0:T(8,128)S(1)}, f32[8,256]{1,0:T(8,128)S(1)}, u32[]{:S(2)}, u32[]{:S(2)}) collective-permute-start(f32[8,256]{1,0:T(8,128)S(1)} %get-tuple-element.87), channel_id=1, source_target_pairs={{0,12},{1,13},{2,14},{3,15},{4,16},{5,17},{6,18},{7,19},{8,20},{9,... | collective-permute-start | bytes 24584 | tf_op jit(solution)/shard_map/ppermute | solution.py:40
  62.7 6.6 %collective-permute-start.16 = (f32[8,256]{1,0:T(8,128)S(1)}, f32[8,256]{1,0:T(8,128)S(1)}, u32[]{:S(2)}, u32[]{:S(2)}) collective-permute-start(f32[8,256]{1,0:T(8,128)S(1)} %get-tuple-element.86.refs_0_), channel_id=1, source_target_pairs={{0,20},{1,21},{2,22},{3,23},{4,24},{5,25},{6,26},{7,27},{8,28},{9,... | collective-permute-start | bytes 24584 | tf_op jit(solution)/shard_map/ppermute | solution.py:40
  69.7 15.3 %collective-permute-start.19 = (bf16[592,256]{1,0:T(8,128)(2,1)S(1)}, bf16[592,256]{1,0:T(8,128)(2,1)S(1)}, u32[]{:S(2)}, u32[]{:S(2)}) collective-permute-start(bf16[592,256]{1,0:T(8,128)(2,1)S(1)} %get-tuple-element.93), channel_id=1, source_target_pairs={{0,32},{1,33},{2,34},{3,35},{4,36},{5,37},{6,38},{7,39},{8,40},{9,... | collective-permute-start | bytes 909320 | tf_op jit(solution)/shard_map/ppermute | solution.py:40
  69.8 20.7 %copy-start = (bf16[272,4096]{1,0:T(8,128)(2,1)S(1)}, bf16[272,4096]{1,0:T(8,128)(2,1)}, u32[]{:S(2)}) copy-start(bf16[272,4096]{1,0:T(8,128)(2,1)} %get-tuple-element.88.h0) | copy-start | bytes 6684676
  77.1 10.7 %collective-permute-start.21 = (bf16[4,32,1024]{2,1,0:T(8,128)(2,1)S(1)}, bf16[4,32,1024]{2,1,0:T(8,128)(2,1)S(1)}, u32[]{:S(2)}, u32[]{:S(2)}) collective-permute-start(bf16[4,32,1024]{2,1,0:T(8,128)(2,1)S(1)} %get-tuple-element.95), channel_id=1, source_target_pairs={{0,2},{1,3},{2,0},{3,1},{4,6},{5,7},{6,4},{7,5},{8,10},{9,11},{10,... | collective-permute-start | bytes 786440 | tf_op jit(solution)/shard_map/ppermute | solution.py:40
  78.6 16.6 %collective-permute-start.22 = (bf16[4,32,1024]{2,1,0:T(8,128)(2,1)S(1)}, bf16[4,32,1024]{2,1,0:T(8,128)(2,1)S(1)}, u32[]{:S(2)}, u32[]{:S(2)}) collective-permute-start(bf16[4,32,1024]{2,1,0:T(8,128)(2,1)S(1)} %get-tuple-element.96), channel_id=1, source_target_pairs={{0,3},{1,0},{2,1},{3,2},{4,7},{5,4},{6,5},{7,6},{8,11},{9,8},{10,9... | collective-permute-start | bytes 786440 | tf_op jit(solution)/shard_map/ppermute | solution.py:40
  81.0 14.2 %collective-permute-start.23 = (bf16[4,32,1024]{2,1,0:T(8,128)(2,1)S(1)}, bf16[4,32,1024]{2,1,0:T(8,128)(2,1)S(1)}, u32[]{:S(2)}, u32[]{:S(2)}) collective-permute-start(bf16[4,32,1024]{2,1,0:T(8,128)(2,1)S(1)} %get-tuple-element.97), channel_id=1, source_target_pairs={{0,192},{1,193},{2,194},{3,195},{4,196},{5,197},{6,198},{7,199},{8... | collective-permute-start | bytes 786440 | tf_op jit(solution)/shard_map/ppermute | solution.py:40
  83.6 11.6 %collective-permute-start.24 = (bf16[4,32,1024]{2,1,0:T(8,128)(2,1)S(1)}, bf16[4,32,1024]{2,1,0:T(8,128)(2,1)S(1)}, u32[]{:S(2)}, u32[]{:S(2)}) collective-permute-start(bf16[4,32,1024]{2,1,0:T(8,128)(2,1)S(1)} %get-tuple-element.98), channel_id=1, source_target_pairs={{0,128},{1,129},{2,130},{3,131},{4,132},{5,133},{6,134},{7,135},{8... | collective-permute-start | bytes 786440 | tf_op jit(solution)/shard_map/ppermute | solution.py:40
  85.0 13.6 %collective-permute-start.25 = (bf16[4,32,1024]{2,1,0:T(8,128)(2,1)S(1)}, bf16[4,32,1024]{2,1,0:T(8,128)(2,1)S(1)}, u32[]{:S(2)}, u32[]{:S(2)}) collective-permute-start(bf16[4,32,1024]{2,1,0:T(8,128)(2,1)S(1)} %get-tuple-element.99), channel_id=1, source_target_pairs={{0,64},{1,65},{2,66},{3,67},{4,68},{5,69},{6,70},{7,71},{8,72},{9,... | collective-permute-start | bytes 786440 | tf_op jit(solution)/shard_map/ppermute | solution.py:40
  87.8 10.8 %collective-permute-start.20 = (bf16[4,32,1024]{2,1,0:T(8,128)(2,1)S(1)}, bf16[4,32,1024]{2,1,0:T(8,128)(2,1)S(1)}, u32[]{:S(2)}, u32[]{:S(2)}) collective-permute-start(bf16[4,32,1024]{2,1,0:T(8,128)(2,1)S(1)} %get-tuple-element.94), channel_id=1, source_target_pairs={{0,1},{1,2},{2,3},{3,0},{4,5},{5,6},{6,7},{7,4},{8,9},{9,10},{10,1... | collective-permute-start | bytes 786440 | tf_op jit(solution)/shard_map/ppermute | solution.py:40
  98.8 6.7 %collective-permute-start.26 = (f32[32,1024]{1,0:T(8,128)S(1)}, f32[32,1024]{1,0:T(8,128)S(1)}, u32[]{:S(2)}, u32[]{:S(2)}) collective-permute-start(f32[32,1024]{1,0:T(8,128)S(1)} %get-tuple-element.116), channel_id=1, source_target_pairs={{0,192},{1,193},{2,194},{3,195},{4,196},{5,197},{6,198},{7,199},{8... | collective-permute-start | bytes 393224 | tf_op jit(solution)/shard_map/ppermute | solution.py:40
  99.7 7.4 %collective-permute-start.27 = (f32[32,1024]{1,0:T(8,128)S(1)}, f32[32,1024]{1,0:T(8,128)S(1)}, u32[]{:S(2)}, u32[]{:S(2)}) collective-permute-start(f32[32,1024]{1,0:T(8,128)S(1)} %get-tuple-element.117), channel_id=1, source_target_pairs={{0,128},{1,129},{2,130},{3,131},{4,132},{5,133},{6,134},{7,135},{8... | collective-permute-start | bytes 393224 | tf_op jit(solution)/shard_map/ppermute | solution.py:40
  101.1 7.8 %collective-permute-start.28 = (f32[32,1024]{1,0:T(8,128)S(1)}, f32[32,1024]{1,0:T(8,128)S(1)}, u32[]{:S(2)}, u32[]{:S(2)}) collective-permute-start(f32[32,1024]{1,0:T(8,128)S(1)} %get-tuple-element.118), channel_id=1, source_target_pairs={{0,64},{1,65},{2,66},{3,67},{4,68},{5,69},{6,70},{7,71},{8,72},{9,... | collective-permute-start | bytes 393224 | tf_op jit(solution)/shard_map/ppermute | solution.py:40
  102.0 7.0 %collective-permute-start.29 = (f32[32,1024]{1,0:T(8,128)S(1)}, f32[32,1024]{1,0:T(8,128)S(1)}, u32[]{:S(2)}, u32[]{:S(2)}) collective-permute-start(f32[32,1024]{1,0:T(8,128)S(1)} %get-tuple-element.120), channel_id=1, source_target_pairs={{0,1},{1,2},{2,3},{3,0},{4,5},{5,6},{6,7},{7,4},{8,9},{9,10},{10,1... | collective-permute-start | bytes 393224 | tf_op jit(solution)/shard_map/ppermute | solution.py:40
  102.2 7.3 %collective-permute-start.30 = (f32[32,1024]{1,0:T(8,128)S(1)}, f32[32,1024]{1,0:T(8,128)S(1)}, u32[]{:S(2)}, u32[]{:S(2)}) collective-permute-start(f32[32,1024]{1,0:T(8,128)S(1)} %get-tuple-element.121), channel_id=1, source_target_pairs={{0,2},{1,3},{2,0},{3,1},{4,6},{5,7},{6,4},{7,5},{8,10},{9,11},{10,... | collective-permute-start | bytes 393224 | tf_op jit(solution)/shard_map/ppermute | solution.py:40
  105.5 5.4 %collective-permute-start.31 = (f32[32,1024]{1,0:T(8,128)S(1)}, f32[32,1024]{1,0:T(8,128)S(1)}, u32[]{:S(2)}, u32[]{:S(2)}) collective-permute-start(f32[32,1024]{1,0:T(8,128)S(1)} %get-tuple-element.122), channel_id=1, source_target_pairs={{0,3},{1,0},{2,1},{3,2},{4,7},{5,4},{6,5},{7,6},{8,11},{9,8},{10,9... | collective-permute-start | bytes 393224 | tf_op jit(solution)/shard_map/ppermute | solution.py:40
  111.5 8.8 %collective-permute-start.32 = (f32[3,64,128]{2,1,0:T(8,128)S(1)}, f32[3,64,128]{2,1,0:T(8,128)S(1)}, u32[]{:S(2)}, u32[]{:S(2)}) collective-permute-start(f32[3,64,128]{2,1,0:T(8,128)S(1)} %get-tuple-element.126), channel_id=1, source_target_pairs={{0,12},{1,13},{2,14},{3,15},{4,16},{5,17},{6,18},{7,19},{8,20},{9,... | collective-permute-start | bytes 294920 | tf_op jit(solution)/shard_map/ppermute | solution.py:40
  114.2 6.1 %collective-permute-start.33 = (f32[2,64,128]{2,1,0:T(8,128)S(1)}, f32[2,64,128]{2,1,0:T(8,128)S(1)}, u32[]{:S(2)}, u32[]{:S(2)}) collective-permute-start(f32[2,64,128]{2,1,0:T(8,128)S(1)} %get-tuple-element.127), channel_id=1, source_target_pairs={{0,20},{1,21},{2,22},{3,23},{4,24},{5,25},{6,26},{7,27},{8,28},{9,... | collective-permute-start | bytes 196616 | tf_op jit(solution)/shard_map/ppermute | solution.py:40
  120.3 6.0 %collective-permute-start.34 = (f32[1,64,128]{2,1,0:T(8,128)S(1)}, f32[1,64,128]{2,1,0:T(8,128)S(1)}, u32[]{:S(2)}, u32[]{:S(2)}) collective-permute-start(f32[1,64,128]{2,1,0:T(8,128)S(1)} %get-tuple-element.129), channel_id=1, source_target_pairs={{0,4},{1,5},{2,6},{3,7},{4,8},{5,9},{6,10},{7,11},{8,12},{9,13},{1... | collective-permute-start | bytes 98312 | tf_op jit(solution)/shard_map/ppermute | solution.py:40
  122.4 5.6 %collective-permute-start.35 = (f32[1,64,128]{2,1,0:T(8,128)S(1)}, f32[1,64,128]{2,1,0:T(8,128)S(1)}, u32[]{:S(2)}, u32[]{:S(2)}) collective-permute-start(f32[1,64,128]{2,1,0:T(8,128)S(1)} %get-tuple-element.130), channel_id=1, source_target_pairs={{0,28},{1,29},{2,30},{3,31},{4,0},{5,1},{6,2},{7,3},{8,4},{9,5},{1... | collective-permute-start | bytes 98312 | tf_op jit(solution)/shard_map/ppermute | solution.py:40
